TPU v7x, 256 devices: a whole 4x4x8 slice. The times are simulated.
256 devices in a mesh: wide: 64 (over z, y, core), narrow: 4 (over x).
Axes of the slice: x: 4, y: 4, z: 8, core: 2. Of those that a mesh axis runs over, the one named last changes fastest.
Arguments:
- soil_state: bfloat16 [4, 5120, 256], P('narrow', 'wide'), may hold values from -0.3125 to 3, as said below
- directions: bfloat16 [4, 5120, 64, 128], P('narrow', 'wide'), may hold values from -6 to 6
- blocks: bfloat16 [4, 5120, 4096], P('narrow', 'wide'), may hold values from -0.75 to 0.75
- send_left: int32 [64], replicated, may hold values from 0 to 8, as said below
- send_right: int32 [64], replicated, may hold values from 0 to 8, as said below
- neighbours: int32 [4, 6, 4096], P('narrow', None, 'wide'), may hold values from -1 to 111, as said below
- face_blocks: bfloat16 [6, 64, 64], replicated, may hold values from -0.75 to 0.75
Outputs:
- second_product: bfloat16 [4, 4096, 64, 128], P('narrow', 'wide')
Inputs may be any that keep to these rules, and one draw needn't show every extreme that they name: `send_left`: the first block sends nothing to the previous one; every other block sends at least one; some block sends exactly 8. `send_right`: the last block sends nothing to the next one; every other block sends at least one; some block sends exactly 8. `neighbours`: faces 0 to 3 are horizontal; positions 64 to 79 appear only outside the first wide block, 80 to 95 only outside the last. Face 4 points up and face 5 down: the element 8 slots before or after in the same block, or the matching element of the bottom or top layer of the sub-tile above or below; -1 at the surface and at the bottom of a column and at some horizontal catchment edges. `soil_state`: pressure heads lie in [-0.3125, -0.1], inverse air-entry values in [0.5, 1], pore indices in [1.4, 2.8], saturated conductivities in [0.3, 3]. Slots of a block beyond its live count hold values of the same ranges.
All inputs are finite; a program needn't handle non-finite values.
Results may differ from a plain program's by a relative error of at most 0.0064.
Values may be sent and summed in bfloat16 or wider, within the bound.
No kernel may reach another device: no remote copies, remote signals or barrier semaphores. Data moves between devices by JAX's collectives and lax.ppermute only.
A program may use at most 64 MiB of HBM per device.

v0:
```python
import jax
import jax.numpy as jnp
from jax import lax
from jax.sharding import PartitionSpec as P

P_SIZE = 64
FACES = 6
NV = 128
E_BAL = 64
MIG = 8
RIM = 16
LAYER = 8


moisture_range = 0.4
time_step = 0.5


def padded(value, sides, width):
    for axis, dim in sides:
        peers, length = (lax.axis_size(axis), value.shape[dim])
        up = [(i, (i + 1) % peers) for i in range(peers - 1)]
        down = [(j, i) for i, j in up]
        last = lax.slice_in_dim(value, length - width, length, axis=dim)
        first = lax.slice_in_dim(value, 0, width, axis=dim)
        before = lax.ppermute(last, axis, up)
        after = lax.ppermute(first, axis, down)
        value = jnp.concatenate([before, value, after], axis=dim)
    return value


def shifted(value, axis, by):
    peers = lax.axis_size(axis)
    pairs = [(i, i + by) for i in range(peers) if 0 <= i + by < peers]
    return lax.ppermute(value, axis, pairs)


def closures(soil_rows):
    soil_float = soil_rows.astype(jnp.float32)
    pressure = soil_float[..., 0:P_SIZE]
    inverse_entry = soil_float[..., P_SIZE : 2 * P_SIZE]
    pore_index = soil_float[..., 2 * P_SIZE : 3 * P_SIZE]
    conduct_sat = soil_float[..., 3 * P_SIZE : 4 * P_SIZE]
    exponent = 1.0 - 1.0 / pore_index
    log_scaled = jnp.log(-inverse_entry * pressure)
    power = jnp.exp(pore_index * log_scaled)
    log_denom = jnp.log1p(power)
    saturation = jnp.exp(-exponent * log_denom)
    ratio_log = pore_index * log_scaled - log_denom
    relative = jnp.sqrt(saturation) * jnp.square(1.0 - jnp.exp(exponent * ratio_log))
    capacity = (
        moisture_range
        * inverse_entry
        * pore_index
        * exponent
        * jnp.exp((pore_index - 1.0) * log_scaled - (exponent + 1.0) * log_denom)
        / time_step
    )
    return (capacity, conduct_sat * relative)


def weigh(weight, vectors):
    return (weight[..., None] * vectors.astype(jnp.float32)).astype(jnp.bfloat16)


def assemble(previous, left_slab, right_slab, arrive_left, arrive_right, mine_left):
    trailing = previous.shape[2:]
    pad_full = jnp.zeros((1, E_BAL) + trailing, previous.dtype)
    pad_move = jnp.zeros((1, MIG) + trailing, previous.dtype)
    leading_part = lax.dynamic_slice_in_dim(
        jnp.concatenate([left_slab, pad_full], 1), MIG - arrive_left, E_BAL, 1
    )
    middle = lax.dynamic_slice_in_dim(
        jnp.concatenate([pad_move, previous], 1), MIG + mine_left - arrive_left, E_BAL, 1
    )
    closing_part = lax.dynamic_slice_in_dim(
        jnp.concatenate([pad_full, right_slab], 1), arrive_right, E_BAL, 1
    )
    slot_index = lax.broadcasted_iota(jnp.int32, (1, E_BAL) + (1,) * len(trailing), 1)
    return jnp.where(
        slot_index < arrive_left,
        leading_part,
        jnp.where(slot_index < E_BAL - arrive_right, middle, closing_part),
    )


def wide_rims(weighted):
    end_rows = jnp.concatenate([weighted[:, :RIM], weighted[:, E_BAL - RIM :]], 1)
    framed = padded(end_rows, (("wide", 1),), RIM)
    return (framed[:, :RIM], framed[:, 3 * RIM :])


def column_layers(weighted):
    end_layers = jnp.concatenate([weighted[:, :LAYER], weighted[:, E_BAL - LAYER :]], 0)
    framed = padded(end_layers, (("narrow", 0),), 1)
    return (framed[0:1], framed[3:4])


def apply_jacobian(
    vectors, weighted, capacity, blocks_new, face_blocks, neighbours, left_rim, right_rim
):
    above_layer, below_layer = column_layers(weighted)
    zero_row = jnp.zeros((1, 1, P_SIZE, NV), jnp.bfloat16)
    buffer_rows = jnp.concatenate(
        [weighted, left_rim, right_rim, above_layer, below_layer, zero_row], 1
    )[0]
    missing = E_BAL + 2 * RIM + 2 * LAYER
    rows_index = jnp.where(neighbours[0] < 0, missing, neighbours[0])
    block_rows = blocks_new[0].reshape(E_BAL, P_SIZE, P_SIZE)
    result = capacity[0][:, :, None] * vectors[0].astype(jnp.float32)
    result = result + jnp.einsum(
        "eij,ejv->eiv", block_rows, weighted[0], preferred_element_type=jnp.float32
    )
    for face_index in range(FACES):
        nearby = jnp.take(buffer_rows, rows_index[face_index], axis=0)
        result = result - jnp.einsum(
            "ij,ejv->eiv", face_blocks[face_index], nearby, preferred_element_type=jnp.float32
        )
    return result.astype(jnp.bfloat16)[None]


def per_device(soil_state, directions, blocks, send_left, send_right, neighbours, face_blocks):
    wide_index = lax.axis_index("wide")
    wide_count = lax.axis_size("wide")
    before_index = jnp.maximum(wide_index - 1, 0)
    after_index = jnp.minimum(wide_index + 1, wide_count - 1)
    mine_left = send_left[wide_index]
    mine_right = send_right[wide_index]
    arrive_left = jnp.where(wide_index > 0, send_right[before_index], 0)
    arrive_right = jnp.where(wide_index < wide_count - 1, send_left[after_index], 0)
    live_rows = E_BAL + mine_left + mine_right - arrive_left - arrive_right
    tail_start = live_rows - MIG
    soil_head = soil_state[:, :MIG]
    direction_head = directions[:, :MIG]
    block_head = blocks[:, :MIG]
    soil_tail = lax.dynamic_slice_in_dim(soil_state, tail_start, MIG, 1)
    direction_tail = lax.dynamic_slice_in_dim(directions, tail_start, MIG, 1)
    block_tail = lax.dynamic_slice_in_dim(blocks, tail_start, MIG, 1)
    from_right = shifted((soil_head, direction_head, block_head), "wide", -1)
    from_left = shifted((soil_tail, direction_tail, block_tail), "wide", 1)
    soil_new = assemble(
        soil_state, from_left[0], from_right[0], arrive_left, arrive_right, mine_left
    )
    directions_new = assemble(
        directions, from_left[1], from_right[1], arrive_left, arrive_right, mine_left
    )
    blocks_new = assemble(blocks, from_left[2], from_right[2], arrive_left, arrive_right, mine_left)
    capacity, weight = closures(soil_new)
    weighted = weigh(weight, directions_new)
    first_rims = wide_rims(weighted)
    first_product = apply_jacobian(
        directions_new,
        weighted,
        capacity,
        blocks_new,
        face_blocks,
        neighbours,
        first_rims[0],
        first_rims[1],
    )
    weighted_next = weigh(weight, first_product)
    second_rims = wide_rims(weighted_next)
    return apply_jacobian(
        first_product,
        weighted_next,
        capacity,
        blocks_new,
        face_blocks,
        neighbours,
        second_rims[0],
        second_rims[1],
    )


def solution(mesh):
    in_specs = (
        P("narrow", "wide", None),
        P("narrow", "wide", None, None),
        P("narrow", "wide", None),
        P(),
        P(),
        P("narrow", None, "wide"),
        P(),
    )
    out_specs = P("narrow", "wide", None, None)
    return jax.shard_map(
        per_device, mesh=mesh, in_specs=in_specs, out_specs=out_specs, check_vma=False
    )
```

profile of v0, /device:TPU:128, one launch (start us, length us, event | category | flops | bytes accessed | tf_op | source)
XLA Modules:
  0.0 115.4 jit_solution(16706823775704396574)
XLA Ops:
  4.8 3.9 %collective-permute-start.1 = (bf16[1,8,256]{2,1,0:T(8,128)(2,1)S(1)}, bf16[1,8,256]{2,1,0:T(8,128)(2,1)S(1)}, u32[]{:S(2)}, u32[]{:S(2)}) collective-permute-start(bf16[1,8,256]{2,1,0:T(8,128)(2,1)S(1)} %get-tuple-element.36), channel_id=1, source_target_pairs={{4,0},{8,4},{12,8},{16,12},{20,16},{24,20},{28,24},{32,28},{36,32}... | collective-permute-start | bytes 12296 | tf_op jit(solution)/shard_map/ppermute | solution.py:35
  8.7 1.9 %collective-permute-start = (bf16[1,8,256]{2,1,0:T(8,128)(2,1)S(1)}, bf16[1,8,256]{2,1,0:T(8,128)(2,1)S(1)}, u32[]{:S(2)}, u32[]{:S(2)}) collective-permute-start(bf16[1,8,256]{2,1,0:T(8,128)(2,1)S(1)} %get-tuple-element.37), channel_id=1, source_target_pairs={{0,4},{4,8},{8,12},{12,16},{16,20},{20,24},{24,28},{28,32},{32,36}... | collective-permute-start | bytes 12296 | tf_op jit(solution)/shard_map/ppermute | solution.py:35
  11.6 7.0 %collective-permute-start.5 = (bf16[1,8,4096]{2,1,0:T(8,128)(2,1)S(1)}, bf16[1,8,4096]{2,1,0:T(8,128)(2,1)S(1)}, u32[]{:S(2)}, u32[]{:S(2)}) collective-permute-start(bf16[1,8,4096]{2,1,0:T(8,128)(2,1)S(1)} %get-tuple-element.32), channel_id=1, source_target_pairs={{4,0},{8,4},{12,8},{16,12},{20,16},{24,20},{28,24},{32,28},{36,32}... | collective-permute-start | bytes 196616 | tf_op jit(solution)/shard_map/ppermute | solution.py:35
  18.5 1.9 %collective-permute-start.4 = (bf16[1,8,4096]{2,1,0:T(8,128)(2,1)S(1)}, bf16[1,8,4096]{2,1,0:T(8,128)(2,1)S(1)}, u32[]{:S(2)}, u32[]{:S(2)}) collective-permute-start(bf16[1,8,4096]{2,1,0:T(8,128)(2,1)S(1)} %get-tuple-element.33), channel_id=1, source_target_pairs={{0,4},{4,8},{8,12},{12,16},{16,20},{20,24},{24,28},{28,32},{32,36}... | collective-permute-start | bytes 196616 | tf_op jit(solution)/shard_map/ppermute | solution.py:35
  21.5 1.9 %collective-permute-start.2 = (bf16[1,8,64,128]{3,2,1,0:T(8,128)(2,1)S(1)}, bf16[1,8,64,128]{3,2,1,0:T(8,128)(2,1)S(1)}, u32[]{:S(2)}, u32[]{:S(2)}) collective-permute-start(bf16[1,8,64,128]{3,2,1,0:T(8,128)(2,1)S(1)} %get-tuple-element.22), channel_id=1, source_target_pairs={{0,4},{4,8},{8,12},{12,16},{16,20},{20,24},{24,28},{28,32},{32,36}... | collective-permute-start | bytes 393224 | tf_op jit(solution)/shard_map/ppermute | solution.py:35
  24.8 7.0 %collective-permute-start.3 = (bf16[1,8,64,128]{3,2,1,0:T(8,128)(2,1)S(1)}, bf16[1,8,64,128]{3,2,1,0:T(8,128)(2,1)S(1)}, u32[]{:S(2)}, u32[]{:S(2)}) collective-permute-start(bf16[1,8,64,128]{3,2,1,0:T(8,128)(2,1)S(1)} %get-tuple-element.23), channel_id=1, source_target_pairs={{4,0},{8,4},{12,8},{16,12},{20,16},{24,20},{28,24},{32,28},{36,32}... | collective-permute-start | bytes 393224 | tf_op jit(solution)/shard_map/ppermute | solution.py:35
  34.3 2.1 %reshape_squeeze.4 = bf16[64,64,64]{2,1,0:T(8,128)(2,1)} reshape(bf16[1,64,4096]{2,1,0:T(8,128)(2,1)S(1)} %fusion.61) | data formatting | bytes 1048576 | tf_op jit(solution)/shard_map/reshape;squeeze | solution.py:109
  36.4 1.7 %fusion.18 = (bf16[1,64,64,128]{3,2,1,0:T(8,128)(2,1)S(1)}, bf16[1,64,64,128]{3,2,1,0:T(8,128)(2,1)S(1)}) fusion(f32[64,64]{1,0:T(8,128)S(1)} %get-tuple-element.35, s32[]{:T(128)S(6)} %select_n.75, bf16[1,8,64,128]{3,2,1,0:T(8,128)(2,1)S(1)} %collective-permute-done.3, s32[]{:T(128)S(6)} %select_n.74, bf16[1,80,64,128]{3,2,1,0:T(8,128)(2,1)S(1)} %copy-done.13, ...), kind=kLoop, calls=%fused_computation.34 | loop fusion | flops 2621440 | bytes 3686540 | tf_op jit(solution)/shard_map/convert_element_type | solution.py:63
  39.5 4.6 %collective-permute-start.8 = (bf16[1,8,64,128]{3,2,1,0:T(8,128)(2,1)S(1)}, bf16[1,8,64,128]{3,2,1,0:T(8,128)(2,1)S(1)}, u32[]{:S(2)}, u32[]{:S(2)}) collective-permute-start(bf16[1,8,64,128]{3,2,1,0:T(8,128)(2,1)S(1)} %get-tuple-element.29), channel_id=1, source_target_pairs={{0,1},{1,2},{2,3},{4,5},{5,6},{6,7},{8,9},{9,10},{10,11},{12,13},{... | collective-permute-start | bytes 393224 | tf_op jit(solution)/shard_map/ppermute | solution.py:26
  44.0 4.4 %collective-permute-start.7 = (bf16[1,16,64,128]{3,2,1,0:T(8,128)(2,1)S(1)}, bf16[1,16,64,128]{3,2,1,0:T(8,128)(2,1)S(1)}, u32[]{:S(2)}, u32[]{:S(2)}) collective-permute-start(bf16[1,16,64,128]{3,2,1,0:T(8,128)(2,1)S(1)} %get-tuple-element.30), channel_id=1, source_target_pairs={{4,0},{8,4},{12,8},{16,12},{20,16},{24,20},{28,24},{32,28},{36,32}... | collective-permute-start | bytes 786440 | tf_op jit(solution)/shard_map/ppermute | solution.py:27
  48.4 1.9 %collective-permute-start.6 = (bf16[1,16,64,128]{3,2,1,0:T(8,128)(2,1)S(1)}, bf16[1,16,64,128]{3,2,1,0:T(8,128)(2,1)S(1)}, u32[]{:S(2)}, u32[]{:S(2)}) collective-permute-start(bf16[1,16,64,128]{3,2,1,0:T(8,128)(2,1)S(1)} %get-tuple-element.31), channel_id=1, source_target_pairs={{0,4},{4,8},{8,12},{12,16},{16,20},{20,24},{24,28},{28,32},{32,36}... | collective-permute-start | bytes 786440 | tf_op jit(solution)/shard_map/ppermute | solution.py:26
  51.1 8.4 %collective-permute-done.6 = bf16[1,16,64,128]{3,2,1,0:T(8,128)(2,1)S(1)} collective-permute-done((bf16[1,16,64,128]{3,2,1,0:T(8,128)(2,1)S(1)}, bf16[1,16,64,128]{3,2,1,0:T(8,128)(2,1)S(1)}, u32[]{:S(2)}, u32[]{:S(2)}) %collective-permute-start.6) | collective-permute-done | bytes 262176 | tf_op jit(solution)/shard_map/ppermute | solution.py:26
  61.3 1.7 %gather_fusion.4 = bf16[64,64,128]{2,1,0:T(8,128)(2,1)} fusion(bf16[113,64,128]{2,1,0:T(8,128)(2,1)S(1)} %bitcast.139, s32[1024]{0:T(1024)S(1)} %get-tuple-element.55), kind=kCustom, calls=%fused_computation.4.clone | custom fusion | bytes 2097408 | tf_op jit(solution)/shard_map/jit(_take)/gather | solution.py:115
  68.0 1.7 %gather_fusion = bf16[64,64,128]{2,1,0:T(8,128)(2,1)} fusion(bf16[113,64,128]{2,1,0:T(8,128)(2,1)S(1)} %bitcast.143, s32[1024]{0:T(1024)S(1)} %get-tuple-element.59), kind=kCustom, calls=%fused_computation.clone | custom fusion | bytes 2097408 | tf_op jit(solution)/shard_map/jit(_take)/gather | solution.py:115
  69.7 1.8 %fusion.35 = f32[64,128,64]{1,2,0:T(8,128)S(1)} fusion(bf16[64,64,128]{2,1,0:T(8,128)(2,1)} %gather_fusion.5, pred[64]{0:T(512)(128)(4,1)S(1)} %get-tuple-element.38, bf16[6,64,64]{2,1,0:T(8,128)(2,1)S(1)} %copy-done.14), kind=kOutput, calls=%fused_computation.54 | convolution fusion | flops 67633152 | bytes 3162624 | tf_op jit(solution)/shard_map/ij,ejv->eiv/dot_general | solution.py:116
  78.8 1.9 %collective-permute-start.10 = (bf16[1,16,64,128]{3,2,1,0:T(8,128)(2,1)S(1)}, bf16[1,16,64,128]{3,2,1,0:T(8,128)(2,1)S(1)}, u32[]{:S(2)}, u32[]{:S(2)}) collective-permute-start(bf16[1,16,64,128]{3,2,1,0:T(8,128)(2,1)S(1)} %get-tuple-element.27), channel_id=1, source_target_pairs={{0,4},{4,8},{8,12},{12,16},{16,20},{20,24},{24,28},{28,32},{32,36}... | collective-permute-start | bytes 786440 | tf_op jit(solution)/shard_map/ppermute | solution.py:26
  80.7 7.0 %collective-permute-start.11 = (bf16[1,16,64,128]{3,2,1,0:T(8,128)(2,1)S(1)}, bf16[1,16,64,128]{3,2,1,0:T(8,128)(2,1)S(1)}, u32[]{:S(2)}, u32[]{:S(2)}) collective-permute-start(bf16[1,16,64,128]{3,2,1,0:T(8,128)(2,1)S(1)} %get-tuple-element.26), channel_id=1, source_target_pairs={{4,0},{8,4},{12,8},{16,12},{20,16},{24,20},{28,24},{32,28},{36,32}... | collective-permute-start | bytes 786440 | tf_op jit(solution)/shard_map/ppermute | solution.py:27
  89.0 4.7 %collective-permute-start.12 = (bf16[1,8,64,128]{3,2,1,0:T(8,128)(2,1)S(1)}, bf16[1,8,64,128]{3,2,1,0:T(8,128)(2,1)S(1)}, u32[]{:S(2)}, u32[]{:S(2)}) collective-permute-start(bf16[1,8,64,128]{3,2,1,0:T(8,128)(2,1)S(1)} %get-tuple-element.25), channel_id=1, source_target_pairs={{0,1},{1,2},{2,3},{4,5},{5,6},{6,7},{8,9},{9,10},{10,11},{12,13},{... | collective-permute-start | bytes 393224 | tf_op jit(solution)/shard_map/ppermute | solution.py:26
  93.9 2.2 %collective-permute-done.12 = bf16[1,8,64,128]{3,2,1,0:T(8,128)(2,1)S(1)} collective-permute-done((bf16[1,8,64,128]{3,2,1,0:T(8,128)(2,1)S(1)}, bf16[1,8,64,128]{3,2,1,0:T(8,128)(2,1)S(1)}, u32[]{:S(2)}, u32[]{:S(2)}) %collective-permute-start.12) | collective-permute-done | bytes 131104 | tf_op jit(solution)/shard_map/ppermute | solution.py:26
  98.6 1.7 %gather_fusion.9 = bf16[64,64,128]{2,1,0:T(8,128)(2,1)} fusion(bf16[113,64,128]{2,1,0:T(8,128)(2,1)S(1)} %bitcast.134, s32[1024]{0:T(1024)S(1)} %get-tuple-element.56), kind=kCustom, calls=%fused_computation.9.clone | custom fusion | bytes 2097408 | tf_op jit(solution)/shard_map/jit(_take)/gather | solution.py:115
  101.9 1.7 %gather_fusion.7 = bf16[64,64,128]{2,1,0:T(8,128)(2,1)} fusion(bf16[113,64,128]{2,1,0:T(8,128)(2,1)S(1)} %bitcast.136, s32[1024]{0:T(1024)S(1)} %get-tuple-element.58), kind=kCustom, calls=%fused_computation.7.clone | custom fusion | bytes 2097408 | tf_op jit(solution)/shard_map/jit(_take)/gather | solution.py:115
  103.6 1.7 %gather_fusion.6 = bf16[64,64,128]{2,1,0:T(8,128)(2,1)} fusion(bf16[113,64,128]{2,1,0:T(8,128)(2,1)S(1)} %bitcast.137, s32[1024]{0:T(1024)S(1)} %get-tuple-element.59), kind=kCustom, calls=%fused_computation.6.clone | custom fusion | bytes 2097408 | tf_op jit(solution)/shard_map/jit(_take)/gather | solution.py:115
  105.3 1.8 %fusion.33 = f32[64,128,64]{1,2,0:T(8,128)S(1)} fusion(bf16[64,64,128]{2,1,0:T(8,128)(2,1)} %gather_fusion.6, pred[64]{0:T(512)(128)(4,1)S(1)} %get-tuple-element.8, bf16[6,64,64]{2,1,0:T(8,128)(2,1)S(1)} %copy-done.14), kind=kOutput, calls=%fused_computation.52 | convolution fusion | flops 67633152 | bytes 3162624 | tf_op jit(solution)/shard_map/ij,ejv->eiv/dot_general | solution.py:116
  112.8 2.6 %fusion.19 = bf16[1,64,64,128]{3,2,1,0:T(8,128)(2,1)} fusion(f32[64,128,64]{1,2,0:T(8,128)S(1)} %fusion.23, f32[64,128,64]{1,2,0:T(8,128)S(1)} %fusion.25, f32[64,128,64]{1,2,0:T(8,128)S(1)} %fusion.27, f32[64,128,64]{1,2,0:T(8,128)S(1)} %fusion.29, f32[64,128,64]{1,2,0:T(8,128)S(1)} %fusion.31, f32[64,128,64]{1,2,0:T(8,128)S(1)} %fusion.33, ...), kind=kOutput, calls=%fused_computation.36 | convolution fusion | flops 73924608 | bytes 15237120 | tf_op jit(solution)/shard_map/eij,ejv->eiv/dot_general | solution.py:111
  (92 shorter events, 34.6 us)
Async XLA Ops:
  0.0 36.4 %copy-start.13 = (bf16[1,80,64,128]{3,2,1,0:T(8,128)(2,1)S(1)}, bf16[1,80,64,128]{3,2,1,0:T(8,128)(2,1)}, u32[]{:S(2)}) copy-start(bf16[1,80,64,128]{3,2,1,0:T(8,128)(2,1)} %param.10) | copy-start | bytes 3932164
  4.8 20.1 %collective-permute-start.1 = (bf16[1,8,256]{2,1,0:T(8,128)(2,1)S(1)}, bf16[1,8,256]{2,1,0:T(8,128)(2,1)S(1)}, u32[]{:S(2)}, u32[]{:S(2)}) collective-permute-start(bf16[1,8,256]{2,1,0:T(8,128)(2,1)S(1)} %get-tuple-element.36), channel_id=1, source_target_pairs={{4,0},{8,4},{12,8},{16,12},{20,16},{24,20},{28,24},{32,28},{36,32}... | collective-permute-start | bytes 12296 | tf_op jit(solution)/shard_map/ppermute | solution.py:35
  8.7 23.1 %collective-permute-start = (bf16[1,8,256]{2,1,0:T(8,128)(2,1)S(1)}, bf16[1,8,256]{2,1,0:T(8,128)(2,1)S(1)}, u32[]{:S(2)}, u32[]{:S(2)}) collective-permute-start(bf16[1,8,256]{2,1,0:T(8,128)(2,1)S(1)} %get-tuple-element.37), channel_id=1, source_target_pairs={{0,4},{4,8},{8,12},{12,16},{16,20},{20,24},{24,28},{28,32},{32,36}... | collective-permute-start | bytes 12296 | tf_op jit(solution)/shard_map/ppermute | solution.py:35
  11.6 21.2 %collective-permute-start.5 = (bf16[1,8,4096]{2,1,0:T(8,128)(2,1)S(1)}, bf16[1,8,4096]{2,1,0:T(8,128)(2,1)S(1)}, u32[]{:S(2)}, u32[]{:S(2)}) collective-permute-start(bf16[1,8,4096]{2,1,0:T(8,128)(2,1)S(1)} %get-tuple-element.32), channel_id=1, source_target_pairs={{4,0},{8,4},{12,8},{16,12},{20,16},{24,20},{28,24},{32,28},{36,32}... | collective-permute-start | bytes 196616 | tf_op jit(solution)/shard_map/ppermute | solution.py:35
  18.5 14.3 %collective-permute-start.4 = (bf16[1,8,4096]{2,1,0:T(8,128)(2,1)S(1)}, bf16[1,8,4096]{2,1,0:T(8,128)(2,1)S(1)}, u32[]{:S(2)}, u32[]{:S(2)}) collective-permute-start(bf16[1,8,4096]{2,1,0:T(8,128)(2,1)S(1)} %get-tuple-element.33), channel_id=1, source_target_pairs={{0,4},{4,8},{8,12},{12,16},{16,20},{20,24},{24,28},{28,32},{32,36}... | collective-permute-start | bytes 196616 | tf_op jit(solution)/shard_map/ppermute | solution.py:35
  21.5 14.9 %collective-permute-start.2 = (bf16[1,8,64,128]{3,2,1,0:T(8,128)(2,1)S(1)}, bf16[1,8,64,128]{3,2,1,0:T(8,128)(2,1)S(1)}, u32[]{:S(2)}, u32[]{:S(2)}) collective-permute-start(bf16[1,8,64,128]{3,2,1,0:T(8,128)(2,1)S(1)} %get-tuple-element.22), channel_id=1, source_target_pairs={{0,4},{4,8},{8,12},{12,16},{16,20},{20,24},{24,28},{28,32},{32,36}... | collective-permute-start | bytes 393224 | tf_op jit(solution)/shard_map/ppermute | solution.py:35
  24.8 11.6 %collective-permute-start.3 = (bf16[1,8,64,128]{3,2,1,0:T(8,128)(2,1)S(1)}, bf16[1,8,64,128]{3,2,1,0:T(8,128)(2,1)S(1)}, u32[]{:S(2)}, u32[]{:S(2)}) collective-permute-start(bf16[1,8,64,128]{3,2,1,0:T(8,128)(2,1)S(1)} %get-tuple-element.23), channel_id=1, source_target_pairs={{4,0},{8,4},{12,8},{16,12},{20,16},{24,20},{28,24},{32,28},{36,32}... | collective-permute-start | bytes 393224 | tf_op jit(solution)/shard_map/ppermute | solution.py:35
  38.2 21.4 %collective-permute-start.9 = (bf16[1,8,64,128]{3,2,1,0:T(8,128)(2,1)S(1)}, bf16[1,8,64,128]{3,2,1,0:T(8,128)(2,1)S(1)}, u32[]{:S(2)}, u32[]{:S(2)}) collective-permute-start(bf16[1,8,64,128]{3,2,1,0:T(8,128)(2,1)S(1)} %get-tuple-element.28), channel_id=1, source_target_pairs={{1,0},{2,1},{3,2},{5,4},{6,5},{7,6},{9,8},{10,9},{11,10},{13,12},{... | collective-permute-start | bytes 393224 | tf_op jit(solution)/shard_map/ppermute | solution.py:27
  39.5 20.1 %collective-permute-start.8 = (bf16[1,8,64,128]{3,2,1,0:T(8,128)(2,1)S(1)}, bf16[1,8,64,128]{3,2,1,0:T(8,128)(2,1)S(1)}, u32[]{:S(2)}, u32[]{:S(2)}) collective-permute-start(bf16[1,8,64,128]{3,2,1,0:T(8,128)(2,1)S(1)} %get-tuple-element.29), channel_id=1, source_target_pairs={{0,1},{1,2},{2,3},{4,5},{5,6},{6,7},{8,9},{9,10},{10,11},{12,13},{... | collective-permute-start | bytes 393224 | tf_op jit(solution)/shard_map/ppermute | solution.py:26
  44.0 15.5 %collective-permute-start.7 = (bf16[1,16,64,128]{3,2,1,0:T(8,128)(2,1)S(1)}, bf16[1,16,64,128]{3,2,1,0:T(8,128)(2,1)S(1)}, u32[]{:S(2)}, u32[]{:S(2)}) collective-permute-start(bf16[1,16,64,128]{3,2,1,0:T(8,128)(2,1)S(1)} %get-tuple-element.30), channel_id=1, source_target_pairs={{4,0},{8,4},{12,8},{16,12},{20,16},{24,20},{28,24},{32,28},{36,32}... | collective-permute-start | bytes 786440 | tf_op jit(solution)/shard_map/ppermute | solution.py:27
  48.4 11.0 %collective-permute-start.6 = (bf16[1,16,64,128]{3,2,1,0:T(8,128)(2,1)S(1)}, bf16[1,16,64,128]{3,2,1,0:T(8,128)(2,1)S(1)}, u32[]{:S(2)}, u32[]{:S(2)}) collective-permute-start(bf16[1,16,64,128]{3,2,1,0:T(8,128)(2,1)S(1)} %get-tuple-element.31), channel_id=1, source_target_pairs={{0,4},{4,8},{8,12},{12,16},{16,20},{20,24},{24,28},{28,32},{32,36}... | collective-permute-start | bytes 786440 | tf_op jit(solution)/shard_map/ppermute | solution.py:26
  66.3 3.3 %copy-start.14 = (bf16[6,64,64]{2,1,0:T(8,128)(2,1)S(1)}, bf16[6,64,64]{2,1,0:T(8,128)(2,1)}, u32[]{:S(2)}) copy-start(bf16[6,64,64]{2,1,0:T(8,128)(2,1)} %param.15) | copy-start | bytes 147460
  69.6 1.8 %copy-start.10 = (bf16[64,64,128]{2,1,0:T(8,128)(2,1)S(1)}, bf16[64,64,128]{2,1,0:T(8,128)(2,1)}, u32[]{:S(2)}) copy-start(bf16[64,64,128]{2,1,0:T(8,128)(2,1)} %gather_fusion.4) | copy-start | bytes 3145732
  71.5 1.2 %copy-start.8 = (bf16[64,64,128]{2,1,0:T(8,128)(2,1)S(1)}, bf16[64,64,128]{2,1,0:T(8,128)(2,1)}, u32[]{:S(2)}) copy-start(bf16[64,64,128]{2,1,0:T(8,128)(2,1)} %gather_fusion.3) | copy-start | bytes 3145732
  72.0 1.3 %copy-start.9 = (bf16[64,64,128]{2,1,0:T(8,128)(2,1)S(1)}, bf16[64,64,128]{2,1,0:T(8,128)(2,1)}, u32[]{:S(2)}) copy-start(bf16[64,64,128]{2,1,0:T(8,128)(2,1)} %gather_fusion.2) | copy-start | bytes 3145732
  73.2 1.2 %copy-start.11 = (bf16[64,64,128]{2,1,0:T(8,128)(2,1)S(1)}, bf16[64,64,128]{2,1,0:T(8,128)(2,1)}, u32[]{:S(2)}) copy-start(bf16[64,64,128]{2,1,0:T(8,128)(2,1)} %gather_fusion) | copy-start | bytes 3145732
  73.8 1.3 %copy-start.6 = (bf16[64,64,128]{2,1,0:T(8,128)(2,1)S(1)}, bf16[64,64,128]{2,1,0:T(8,128)(2,1)}, u32[]{:S(2)}) copy-start(bf16[64,64,128]{2,1,0:T(8,128)(2,1)} %gather_fusion.1) | copy-start | bytes 3145732
  74.9 1.3 %copy-start.2 = (bf16[64,64,64]{2,1,0:T(8,128)(2,1)S(1)}, bf16[64,64,64]{2,1,0:T(8,128)(2,1)}, u32[]{:S(2)}) copy-start(bf16[64,64,64]{2,1,0:T(8,128)(2,1)} %reshape_squeeze.4) | copy-start | bytes 1572868
  78.8 15.0 %collective-permute-start.10 = (bf16[1,16,64,128]{3,2,1,0:T(8,128)(2,1)S(1)}, bf16[1,16,64,128]{3,2,1,0:T(8,128)(2,1)S(1)}, u32[]{:S(2)}, u32[]{:S(2)}) collective-permute-start(bf16[1,16,64,128]{3,2,1,0:T(8,128)(2,1)S(1)} %get-tuple-element.27), channel_id=1, source_target_pairs={{0,4},{4,8},{8,12},{12,16},{16,20},{20,24},{24,28},{28,32},{32,36}... | collective-permute-start | bytes 786440 | tf_op jit(solution)/shard_map/ppermute | solution.py:26
  80.7 13.1 %collective-permute-start.11 = (bf16[1,16,64,128]{3,2,1,0:T(8,128)(2,1)S(1)}, bf16[1,16,64,128]{3,2,1,0:T(8,128)(2,1)S(1)}, u32[]{:S(2)}, u32[]{:S(2)}) collective-permute-start(bf16[1,16,64,128]{3,2,1,0:T(8,128)(2,1)S(1)} %get-tuple-element.26), channel_id=1, source_target_pairs={{4,0},{8,4},{12,8},{16,12},{20,16},{24,20},{28,24},{32,28},{36,32}... | collective-permute-start | bytes 786440 | tf_op jit(solution)/shard_map/ppermute | solution.py:27
  87.7 8.4 %collective-permute-start.13 = (bf16[1,8,64,128]{3,2,1,0:T(8,128)(2,1)S(1)}, bf16[1,8,64,128]{3,2,1,0:T(8,128)(2,1)S(1)}, u32[]{:S(2)}, u32[]{:S(2)}) collective-permute-start(bf16[1,8,64,128]{3,2,1,0:T(8,128)(2,1)S(1)} %get-tuple-element.24), channel_id=1, source_target_pairs={{1,0},{2,1},{3,2},{5,4},{6,5},{7,6},{9,8},{10,9},{11,10},{13,12},{... | collective-permute-start | bytes 393224 | tf_op jit(solution)/shard_map/ppermute | solution.py:27
  89.0 7.1 %collective-permute-start.12 = (bf16[1,8,64,128]{3,2,1,0:T(8,128)(2,1)S(1)}, bf16[1,8,64,128]{3,2,1,0:T(8,128)(2,1)S(1)}, u32[]{:S(2)}, u32[]{:S(2)}) collective-permute-start(bf16[1,8,64,128]{3,2,1,0:T(8,128)(2,1)S(1)} %get-tuple-element.25), channel_id=1, source_target_pairs={{0,1},{1,2},{2,3},{4,5},{5,6},{6,7},{8,9},{9,10},{10,11},{12,13},{... | collective-permute-start | bytes 393224 | tf_op jit(solution)/shard_map/ppermute | solution.py:26
  105.3 1.8 %copy-start.12 = (bf16[64,64,128]{2,1,0:T(8,128)(2,1)S(1)}, bf16[64,64,128]{2,1,0:T(8,128)(2,1)}, u32[]{:S(2)}) copy-start(bf16[64,64,128]{2,1,0:T(8,128)(2,1)} %gather_fusion.7) | copy-start | bytes 3145732
  111.3 1.5 %copy-start.3 = (bf16[64,64,64]{2,1,0:T(8,128)(2,1)S(1)}, bf16[64,64,64]{2,1,0:T(8,128)(2,1)}, u32[]{:S(2)}) copy-start(bf16[64,64,64]{2,1,0:T(8,128)(2,1)} %reshape_squeeze.4) | copy-start | bytes 1572868
  (5 other events, 5.9 us)
where the time goes:
time: 118 us; the launch traced here: 115 us
  starting transfers between devices  50.6 us (43%)
  local copies, waits for them, and re-layouts  31.3 us (27%)
  matrix products  12.7 us (11%)
  waiting for transfers between devices  10.6 us (9%)
  other arithmetic  6.29 us (5%)
  between operations  3.81 us (3%)
    ppermute x6, starting transfers between devices, shifted(): return lax.ppermute(value, axis, pairs)  23.6 us
    gather x12, local copies, waits for them, and re-layouts, apply_jacobian(): nearby = jnp.take(buffer_rows, rows_index[face_index], axis=0)  19.1 us
    ppermute x4, starting transfers between devices, padded(): after = lax.ppermute(first, axis, down)  13.9 us
    ppermute x4, starting transfers between devices, padded(): before = lax.ppermute(last, axis, up)  13.1 us
    ppermute x4, waiting for transfers between devices, padded(): before = lax.ppermute(last, axis, up)  10.6 us
    dot_general x12, matrix products, apply_jacobian(): jnp.einsum('ij,ejv->eiv', face_blocks[face_index], nearby, preferred_elem...  8.51 us
    unnamed x38, local copies, waits for them, and re-layouts  5.83 us
    dot_general x2, matrix products, apply_jacobian(): jnp.einsum('eij,ejv->eiv', block_rows, weighted[0], preferred_element_typ...  4.22 us
  transfers between devices with their start and end apart: 14, of which 2 were waited for; matrix products, arithmetic and copies ran while one was open for 7% of the time, Pallas kernels for 0%

commit v1 on v0

v1 whole, which is shorter than its diff:
```python
import jax
import jax.numpy as jnp
from jax import lax
from jax.experimental import pallas as pl
from jax.experimental.pallas import tpu as pltpu
from jax.sharding import PartitionSpec as P

P_SIZE = 64
FACES = 6
NV = 128
E_BAL = 64
MIG = 8
RIM = 16
LAYER = 8
E_DEV = 80
N_WIDE = 64
COLS = 4
HALF = P_SIZE // 2
ABOVE = E_BAL + 2 * RIM
BELOW = ABOVE + LAYER
MISSING = BELOW + LAYER

DIR_AT = RIM * P_SIZE
BLK_AT = DIR_AT + MIG * P_SIZE
SOIL_AT = BLK_AT + MIG * HALF
MESSAGE = SOIL_AT + 2 * MIG

moisture_range = 0.4
time_step = 0.5

F32 = jnp.float32
BF16 = jnp.bfloat16


def closures(pressure, inverse_entry, pore_index, conduct_sat):
    exponent = 1.0 - 1.0 / pore_index
    log_scaled = jnp.log(-inverse_entry * pressure)
    power = jnp.exp(pore_index * log_scaled)
    log_denom = jnp.log1p(power)
    saturation = jnp.exp(-exponent * log_denom)
    ratio_log = pore_index * log_scaled - log_denom
    relative = jnp.sqrt(saturation) * jnp.square(1.0 - jnp.exp(exponent * ratio_log))
    capacity = (
        moisture_range
        * inverse_entry
        * pore_index
        * exponent
        * jnp.exp((pore_index - 1.0) * log_scaled - (exponent + 1.0) * log_denom)
        / time_step
    )
    return capacity, conduct_sat * relative


def closures_by_column(soil_rows):
    cols = [jnp.transpose(soil_rows[k * NV : (k + 1) * NV]) for k in range(2)]
    fields = [cols[i // 2][i % 2 * P_SIZE : (i % 2 + 1) * P_SIZE] for i in range(4)]
    return closures(*fields)


def counts(send_left, send_right):
    t = lax.axis_index("wide")
    before = lax.rem(t + N_WIDE - 1, N_WIDE)
    after = lax.rem(t + 1, N_WIDE)
    mine_left = send_left[t]
    mine_right = send_right[t]
    arrive_left = jnp.where(t > 0, send_right[before], 0)
    arrive_right = jnp.where(t < N_WIDE - 1, send_left[after], 0)
    live = E_BAL + mine_left + mine_right - arrive_left - arrive_right
    return mine_left, mine_right, arrive_left, arrive_right, live


def rows(index, size=P_SIZE, base=0):
    if isinstance(index, int):
        return pl.ds(base + index * size, size)
    return pl.ds(pl.multiple_of(base + index * size, 16), size)


def wide_column(columns, lane):
    return jnp.broadcast_to(columns[:, lane : lane + 1], (P_SIZE, NV))


def lane_is(p):
    return (lax.broadcasted_iota(jnp.int32, (1, NV), 1) >= P_SIZE) == bool(p)


def prepare_kernel(sl, sr, soil, dirs, blocks, to_right, to_left, cap_out, wt_out, soil_f, blk_f, wb):
    mine_left, mine_right, arrive_left, arrive_right, live = counts(sl, sr)
    for k in range(2):
        soil_f[k * NV : k * NV + E_DEV, :] = soil[:, k * NV : (k + 1) * NV].astype(F32)
        soil_f[k * NV + E_DEV : (k + 1) * NV, :] = jnp.full((NV - E_DEV, NV), 1.0, F32)
    capacity, weight = closures_by_column(soil_f[...])
    cap_out[...] = capacity
    wt_out[...] = weight
    for s in range(E_DEV):
        if s < 24 or s >= 40:
            wb[rows(s), :] = wide_column(weight, s)
    tail = live - MIG
    group = jnp.minimum(lax.div(tail, 16) * 16, E_DEV - 32)
    for g in range(3):
        for c in range(HALF):
            lanes = slice(c * NV, (c + 1) * NV)
            if g == 0:
                x = blocks[0:16, lanes]
            else:
                x = blocks[pl.ds(pl.multiple_of(group + 16 * (g - 1), 16), 16), lanes]
            blk_f[pl.ds(g * 16 * HALF + c, 16, stride=HALF), :] = x.astype(F32)
    middle = mine_left - arrive_left
    for i in range(RIM):
        s = middle + E_BAL - RIM + i
        to_right[rows(i), :] = (wb[rows(s), :] * dirs[rows(s), :].astype(F32)).astype(BF16)
        s = jnp.maximum(middle + i, 0)
        to_left[rows(i), :] = (wb[rows(s), :] * dirs[rows(s), :].astype(F32)).astype(BF16)
    to_right[pl.ds(DIR_AT, MIG * P_SIZE), :] = dirs[pl.ds(pl.multiple_of(tail * P_SIZE, P_SIZE), MIG * P_SIZE), :]
    to_left[pl.ds(DIR_AT, MIG * P_SIZE), :] = dirs[0 : MIG * P_SIZE, :]
    at = pl.multiple_of((16 + tail - group) * HALF, HALF)
    to_right[pl.ds(BLK_AT, MIG * HALF), :] = blk_f[pl.ds(at, MIG * HALF), :].astype(BF16)
    to_left[pl.ds(BLK_AT, MIG * HALF), :] = blk_f[0 : MIG * HALF, :].astype(BF16)
    for out, first in ((to_right, tail), (to_left, 0)):
        both = jnp.concatenate([soil_f[pl.ds(k * NV + first, MIG), :] for k in range(2)], 0)
        out[pl.ds(SOIL_AT, 2 * MIG), :] = both.astype(BF16)


def own_kernel(wt, dirs, blocks, weighted, matrices, blk_f):
    weight = wt[...]
    for s in range(E_DEV):
        weighted[rows(s), :] = (wide_column(weight, s) * dirs[rows(s), :].astype(F32)).astype(BF16)
    for g in range(E_DEV // 16):
        for c in range(HALF):
            x = blocks[g * 16 : (g + 1) * 16, c * NV : (c + 1) * NV].astype(F32)
            for p in range(2):
                blk_f[pl.ds(2 * c + p, 16, stride=P_SIZE), :] = jnp.where(lane_is(p), x, 0.0)
        matrices[g * 16 * P_SIZE : (g + 1) * 16 * P_SIZE, :] = blk_f[...].astype(BF16)


def arrive_kernel(sl, sr, cap_own, wt_own, soil_l, soil_r, dir_l, dir_r, own, to_above, to_below, moved, cap_out, wt_out, soil_f):
    mine_left, mine_right, arrive_left, arrive_right, live = counts(sl, sr)
    soil_f[...] = jnp.full((2 * NV, NV), 1.0, F32)
    for side, ref in enumerate((soil_l, soil_r)):
        x = ref[...].astype(F32)
        for k in range(2):
            soil_f[k * NV + side * MIG : k * NV + (side + 1) * MIG, :] = x[k * MIG : (k + 1) * MIG]
    capacity, weight = closures_by_column(soil_f[...])
    lane = lax.broadcasted_iota(jnp.int32, (P_SIZE, NV), 1)
    for out, mine, theirs in ((cap_out, cap_own, capacity), (wt_out, wt_own, weight)):
        middle = pltpu.roll(mine[...], lax.rem(arrive_left - mine_left + NV, NV), 1)
        left = pltpu.roll(theirs, lax.rem(arrive_left - MIG + NV, NV), 1)
        right = pltpu.roll(theirs, E_BAL - arrive_right - MIG, 1)
        out[...] = jnp.where(lane < arrive_left, left, jnp.where(lane < E_BAL - arrive_right, middle, right))
    for i in range(MIG):
        moved[rows(i), :] = (wide_column(weight, i) * dir_l[rows(i), :].astype(F32)).astype(BF16)
        moved[rows(MIG + i), :] = (wide_column(weight, MIG + i) * dir_r[rows(i), :].astype(F32)).astype(BF16)
    shift = mine_left - arrive_left
    for i in range(LAYER):
        here = own[rows(jnp.maximum(shift + i, 0)), :].astype(F32)
        came = moved[rows(jnp.minimum(MIG - arrive_left + i, MIG - 1)), :].astype(F32)
        to_above[rows(i), :] = jnp.where(i < arrive_left, came, here).astype(BF16)
        w = E_BAL - LAYER + i
        here = own[rows(shift + w), :].astype(F32)
        came = moved[rows(jnp.maximum(w - E_BAL + arrive_right, 0) + MIG), :].astype(F32)
        to_below[rows(i), :] = jnp.where(w >= E_BAL - arrive_right, came, here).astype(BF16)


def first_kernel(
    sl, sr, nbr, cap, wt, faces, dirs, own, matrices, moved, above, below, from_left, from_right,
    near, blk_out, partial, first, nxt, blk_f,
):
    mine_left, mine_right, arrive_left, arrive_right, live = counts(sl, sr)
    shift = mine_left - arrive_left
    for w in range(E_BAL):
        if w < LAYER:
            near[rows(w), :] = above[rows(w), :]
        elif w >= E_BAL - LAYER:
            near[rows(w), :] = below[rows(w - E_BAL + LAYER), :]
        else:
            near[rows(w), :] = own[rows(shift + w), :]
    for i in range(RIM):
        near[rows(E_BAL + i), :] = from_left[rows(i), :]
        near[rows(E_BAL + RIM + i), :] = from_right[rows(i), :]
    for i in range(MIG):

        @pl.when(i < mine_left)
        def _():
            near[rows(E_BAL + RIM - mine_left + i), :] = own[rows(i), :]

        @pl.when(i < mine_right)
        def _():
            near[rows(E_BAL + RIM + i), :] = own[rows(live - mine_right + i), :]

    near[rows(ABOVE), :] = jnp.zeros((P_SIZE, NV), BF16)

    for w in range(E_BAL):
        blk_out[rows(w), :] = matrices[rows(jnp.maximum(shift + w, 0)), :]
    for i in range(MIG):

        @pl.when(i < arrive_left)
        def _():
            x = from_left[rows(MIG - arrive_left + i, HALF, BLK_AT), :].astype(F32)
            for p in range(2):
                blk_f[pl.ds(p, HALF, stride=2), :] = jnp.where(lane_is(p), x, 0.0)
            blk_out[rows(i), :] = blk_f[...].astype(BF16)

        @pl.when(i < arrive_right)
        def _():
            x = from_right[rows(i, HALF, BLK_AT), :].astype(F32)
            for p in range(2):
                blk_f[pl.ds(p, HALF, stride=2), :] = jnp.where(lane_is(p), x, 0.0)
            blk_out[rows(E_BAL - arrive_right + i), :] = blk_f[...].astype(BF16)

    capacity = cap[...]
    weight = wt[...]
    face_rows = faces[...]
    for w in range(E_BAL):
        vector = dirs[rows(jnp.maximum(shift + w, 0)), :].astype(F32)
        if w < MIG:
            came = from_left[rows(jnp.minimum(MIG - arrive_left + w, MIG - 1), base=DIR_AT), :].astype(F32)
            vector = jnp.where(w < arrive_left, came, vector)
        elif w >= E_BAL - MIG:
            came = from_right[rows(jnp.maximum(w - E_BAL + arrive_right, 0), base=DIR_AT), :].astype(F32)
            vector = jnp.where(w >= E_BAL - arrive_right, came, vector)
        result = wide_column(capacity, w) * vector + product(near, nbr, blk_out, face_rows, w, ABOVE, ABOVE)
        if LAYER <= w < E_BAL - LAYER:
            rounded = result.astype(BF16)
            first[rows(w - LAYER), :] = rounded
            nxt[rows(w - LAYER), :] = (wide_column(weight, w) * rounded.astype(F32)).astype(BF16)
        else:
            partial[rows(w if w < LAYER else w - E_BAL + 2 * LAYER), :] = result


def product(near, nbr, matrices, face_rows, w, limit, missing):
    mine = near[rows(w), :]
    parts = [mine, mine]
    for k in range(FACES):
        b = nbr[k, w]
        b = jnp.where((b < 0) | (b >= limit), missing, b)
        parts.append(near[rows(b), :])
    lhs = jnp.concatenate([matrices[rows(w), :], face_rows], 1)
    return jnp.dot(lhs, jnp.concatenate(parts, 0), preferred_element_type=F32)


def ends_kernel(nbr, wt, faces, partial, from_above, from_below, nxt, first, to_right, to_left, to_above, to_below):
    weight = wt[...]
    for i in range(2 * LAYER):
        top = i < LAYER
        w = i if top else E_BAL - 2 * LAYER + i
        k = 4 if top else 5
        came = from_above if top else from_below
        b = nbr[k, w]
        inside = b - (ABOVE if top else BELOW)
        there = (inside >= 0) & (inside < LAYER)
        row = came[rows(jnp.clip(inside, 0, LAYER - 1)), :]
        update = jnp.dot(faces[:, k * P_SIZE : (k + 1) * P_SIZE], row, preferred_element_type=F32)
        rounded = (partial[rows(i), :] + jnp.where(there, update, 0.0)).astype(BF16)
        first[rows(i), :] = rounded
        onward = (wide_column(weight, w) * rounded.astype(F32)).astype(BF16)
        if top:
            to_left[rows(i), :] = onward
            to_above[rows(i), :] = onward
        else:
            to_right[rows(i), :] = onward
            to_below[rows(i - LAYER), :] = onward
    span = LAYER * P_SIZE
    to_left[span : 2 * span, :] = nxt[0:span, :]
    to_right[0:span, :] = nxt[(E_BAL - 3 * LAYER) * P_SIZE : (E_BAL - 2 * LAYER) * P_SIZE, :]


def second_kernel(
    nbr, cap, faces, matrices, mid, ends, nxt, sent_left, sent_right, from_left, from_right, from_above, from_below,
    out, near,
):
    near[0 : RIM * P_SIZE, :] = sent_left[...]
    near[RIM * P_SIZE : (E_BAL - RIM) * P_SIZE, :] = nxt[LAYER * P_SIZE : (E_BAL - RIM - LAYER) * P_SIZE, :]
    near[(E_BAL - RIM) * P_SIZE : E_BAL * P_SIZE, :] = sent_right[...]
    near[E_BAL * P_SIZE : (E_BAL + RIM) * P_SIZE, :] = from_left[...]
    near[(E_BAL + RIM) * P_SIZE : ABOVE * P_SIZE, :] = from_right[...]
    near[ABOVE * P_SIZE : BELOW * P_SIZE, :] = from_above[...]
    near[BELOW * P_SIZE : MISSING * P_SIZE, :] = from_below[...]
    near[rows(MISSING), :] = jnp.zeros((P_SIZE, NV), BF16)
    capacity = cap[...]
    face_rows = faces[...]
    for w in range(E_BAL):
        if w < LAYER:
            vector = ends[rows(w), :]
        elif w >= E_BAL - LAYER:
            vector = ends[rows(w - E_BAL + 2 * LAYER), :]
        else:
            vector = mid[rows(w - LAYER), :]
        result = wide_column(capacity, w) * vector.astype(F32) + product(
            near, nbr, matrices, face_rows, w, MISSING, MISSING
        )
        out[rows(w), :] = result.astype(BF16)


def smem():
    return pl.BlockSpec(memory_space=pltpu.SMEM)


def vmem():
    return pl.BlockSpec(memory_space=pltpu.VMEM)


def shape(n, kind=BF16):
    return jax.ShapeDtypeStruct((n, NV), kind)


def call(kernel, name, scalars, arrays, outs, scratch=(), flops=0, moved=0):
    return pl.pallas_call(
        kernel,
        out_shape=outs,
        in_specs=[smem()] * len(scalars) + [vmem()] * len(arrays),
        out_specs=[vmem()] * len(outs),
        scratch_shapes=list(scratch),
        compiler_params=pltpu.CompilerParams(vmem_limit_bytes=40 * 2**20),
        cost_estimate=pl.CostEstimate(flops=flops, bytes_accessed=moved, transcendentals=0),
        name=name,
    )(*scalars, *arrays)


def shifted(value, axis, by):
    peers = lax.axis_size(axis)
    return lax.ppermute(value, axis, [(i, (i + by) % peers) for i in range(peers)])


def per_device(soil_state, directions, blocks, send_left, send_right, neighbours, face_blocks):
    soil = soil_state[0]
    dirs = directions.reshape(E_DEV * P_SIZE, NV)
    rows_of = blocks[0]
    nbr = neighbours[0]
    faces = -jnp.swapaxes(face_blocks, 0, 1).reshape(P_SIZE, FACES * P_SIZE)
    column = shape(P_SIZE, F32)

    to_right, to_left, cap_own, wt_own = call(
        prepare_kernel, "prepare", (send_left, send_right), (soil, dirs, rows_of),
        (shape(MESSAGE), shape(MESSAGE), column, column),
        (pltpu.VMEM((2 * NV, NV), F32), pltpu.VMEM((48 * HALF, NV), F32), pltpu.VMEM((E_DEV * P_SIZE, NV), F32)),
    )
    from_left = shifted(to_right, "wide", 1)
    from_right = shifted(to_left, "wide", -1)

    own, matrices = call(
        own_kernel, "own", (), (wt_own, dirs, rows_of),
        (shape(E_DEV * P_SIZE), shape(E_DEV * P_SIZE)),
        (pltpu.VMEM((16 * P_SIZE, NV), F32),),
        flops=10**9, moved=6 * 2**20,
    )

    soil_l, soil_r = from_left[SOIL_AT:], from_right[SOIL_AT:]
    dir_l, dir_r = from_left[DIR_AT:BLK_AT], from_right[DIR_AT:BLK_AT]
    above, below, moved, cap, wt = call(
        arrive_kernel, "arrive", (send_left, send_right), (cap_own, wt_own, soil_l, soil_r, dir_l, dir_r, own),
        (shape(LAYER * P_SIZE), shape(LAYER * P_SIZE), shape(2 * MIG * P_SIZE), column, column),
        (pltpu.VMEM((2 * NV, NV), F32),),
    )
    from_below = shifted(above, "narrow", -1)
    from_above = shifted(below, "narrow", 1)

    near, blk, partial, first, nxt = call(
        first_kernel, "first", (send_left, send_right, nbr),
        (cap, wt, faces, dirs, own, matrices, moved, above, below, from_left, from_right),
        (
            shape((ABOVE + 1) * P_SIZE), shape(E_BAL * P_SIZE), shape(2 * LAYER * P_SIZE, F32),
            shape((E_BAL - 2 * LAYER) * P_SIZE), shape((E_BAL - 2 * LAYER) * P_SIZE),
        ),
        (pltpu.VMEM((P_SIZE, NV), F32),),
        flops=2 * 10**9, moved=8 * 2**20,
    )
    ends, go_right, go_left, go_above, go_below = call(
        ends_kernel, "ends", (nbr,), (wt, faces, partial, from_above, from_below, nxt),
        (
            shape(2 * LAYER * P_SIZE), shape(RIM * P_SIZE), shape(RIM * P_SIZE),
            shape(LAYER * P_SIZE), shape(LAYER * P_SIZE),
        ),
    )
    came_below = shifted(go_above, "narrow", -1)
    came_above = shifted(go_below, "narrow", 1)
    came_left = shifted(go_right, "wide", 1)
    came_right = shifted(go_left, "wide", -1)
    (out,) = call(
        second_kernel, "second", (nbr,),
        (cap, faces, blk, first, ends, nxt, go_left, go_right, came_left, came_right, came_above, came_below),
        (shape(E_BAL * P_SIZE),),
        (pltpu.VMEM(((MISSING + 1) * P_SIZE, NV), BF16),),
        flops=10**9, moved=6 * 2**20,
    )
    return out.reshape(1, E_BAL, P_SIZE, NV)


def solution(mesh):
    in_specs = (
        P("narrow", "wide", None),
        P("narrow", "wide", None, None),
        P("narrow", "wide", None),
        P(),
        P(),
        P("narrow", None, "wide"),
        P(),
    )
    out_specs = P("narrow", "wide", None, None)
    return jax.shard_map(
        per_device, mesh=mesh, in_specs=in_specs, out_specs=out_specs, check_vma=False
    )
```

time: 118 us -> 45.9 us (0.39)
  the two profiles are of different devices: /device:TPU:128 before, /device:TPU:6 now
where the time goes in v1:
time: 45.9 us; the launch traced here: 45.7 us
  starting transfers between devices  17 us (37%)
  Pallas kernels  14.8 us (32%)
  waiting for transfers between devices  6.47 us (14%)
  local copies, waits for them, and re-layouts  6.33 us (14%)
  other arithmetic  0.91 us (2%)
    ppermute x8, starting transfers between devices, shifted(): lax.ppermute(value, axis, [(i, (i + by) % peers) for i in range(peers)])  17 us
    pallas_call x6, Pallas kernels, call(): pl.pallas_call(kernel, out_shape=outs, in_specs=[smem()] * len(scalars) +...  14.8 us
    ppermute x8, waiting for transfers between devices, shifted(): lax.ppermute(value, axis, [(i, (i + by) % peers) for i in range(peers)])  6.47 us
    unnamed x21, local copies, waits for them, and re-layouts  4.53 us
    neg x2, local copies, waits for them, and re-layouts, per_device(): faces = -jnp.swapaxes(face_blocks, 0, 1).reshape(P_SIZE, FACES * P_SIZE)  1.77 us
  transfers between devices with their start and end apart: 8, of which 4 were waited for; matrix products, arithmetic and copies ran while one was open for 6% of the time, Pallas kernels for 15%

profile of v1, /device:TPU:6, one launch (start us, length us, event | category | flops | bytes accessed | tf_op | source)
XLA Modules:
  0.0 45.7 jit_solution(17212917627237637339)
XLA Ops:
  0.0 1.3 %copy-done = bf16[1,80,64,128]{3,2,1,0:T(8,128)(2,1)S(1)} copy-done((bf16[1,80,64,128]{3,2,1,0:T(8,128)(2,1)S(1)}, bf16[1,80,64,128]{3,2,1,0:T(8,128)(2,1)}, u32[]{:S(2)}) %copy-start) | copy-done | bytes 1310744
  1.3 1.1 %copy-done.2 = bf16[1,80,4096]{2,1,0:T(8,128)(2,1)S(1)} copy-done((bf16[1,80,4096]{2,1,0:T(8,128)(2,1)S(1)}, bf16[1,80,4096]{2,1,0:T(8,128)(2,1)}, u32[]{:S(2)}) %copy-start.2) | copy-done | bytes 655384
  2.4 0.8 %copy-done.4 = bf16[1,80,256]{2,1,0:T(8,128)(2,1)S(1)} copy-done((bf16[1,80,256]{2,1,0:T(8,128)(2,1)S(1)}, bf16[1,80,256]{2,1,0:T(8,128)(2,1)}, u32[]{:S(2)}) %copy-start.4) | copy-done | bytes 40984
  3.2 0.7 %copy-done.5 = s32[64]{0:T(128)S(1)} copy-done((s32[64]{0:T(128)S(1)}, s32[64]{0:T(128)}, u32[]{:S(2)}) %copy-start.5) | copy-done | bytes 280
  3.9 0.7 %copy-done.7 = s32[64]{0:T(128)S(1)} copy-done((s32[64]{0:T(128)S(1)}, s32[64]{0:T(128)}, u32[]{:S(2)}) %copy-start.7) | copy-done | bytes 280
  4.5 2.8 %prepare.1 = (bf16[1808,128]{1,0:T(8,128)(2,1)}, bf16[1808,128]{1,0:T(8,128)(2,1)S(1)}, f32[64,128]{1,0:T(8,128)S(1)}, f32[64,128]{1,0:T(8,128)S(1)}) custom-call(s32[64]{0:T(128)S(1)} %copy-done.5, s32[64]{0:T(128)S(1)} %copy-done.7, bf16[80,256]{1,0:T(8,128)(2,1)S(1)} %bitcast.14, bf16[5120,128]{1,0:T(8,128)(2,1)S(1)} %bitcast.9, bf16[80,4096]{1,0:T(8,128)(2,1)S(1)} %bitcast.12), custom_call_target="tpu_custom_call" | custom-call | tf_op jit(solution)/shard_map/prepare/pallas_call | solution.py:306
  7.4 7.7 %collective-permute-start.1 = (bf16[1808,128]{1,0:T(8,128)(2,1)S(1)}, bf16[1808,128]{1,0:T(8,128)(2,1)S(1)}, u32[]{:S(2)}, u32[]{:S(2)}) collective-permute-start(bf16[1808,128]{1,0:T(8,128)(2,1)S(1)} %get-tuple-element.28), channel_id=1, source_target_pairs={{0,252},{4,0},{8,4},{12,8},{16,12},{20,16},{24,20},{28,24},{32,28}... | collective-permute-start | bytes 1388552 | tf_op jit(solution)/shard_map/ppermute | solution.py:320
  15.1 0.9 %negate_bitcast_fusion = bf16[64,6,64]{2,0,1:T(8,128)(2,1)S(1)} fusion(bf16[6,64,64]{2,1,0:T(8,128)(2,1)} %param.13), kind=kLoop, calls=%fused_computation | loop fusion | flops 24576 | bytes 98304 | tf_op jit(solution)/shard_map/neg | solution.py:328
  16.0 0.7 %copy.9 = bf16[64,6,64]{2,1,0:T(8,128)(2,1)} copy(bf16[64,6,64]{2,0,1:T(8,128)(2,1)S(1)} %negate_bitcast_fusion) | data formatting | bytes 98304 | tf_op jit(solution)/shard_map/neg | solution.py:328
  16.7 1.1 %neg.9.faces = bf16[64,384]{1,0:T(8,128)(2,1)S(1)} reshape(bf16[64,6,64]{2,1,0:T(8,128)(2,1)} %copy.9) | data formatting | bytes 98304 | tf_op jit(solution)/shard_map/neg | solution.py:328
  17.8 3.0 %own.1 = (bf16[5120,128]{1,0:T(8,128)(2,1)S(1)}, bf16[5120,128]{1,0:T(8,128)(2,1)S(1)}) custom-call(f32[64,128]{1,0:T(8,128)S(1)} %get-tuple-element.26.wt.wt_own, bf16[5120,128]{1,0:T(8,128)(2,1)S(1)} %bitcast.10, bf16[80,4096]{1,0:T(8,128)(2,1)S(1)} %bitcast.13), custom_call_target="tpu_custom_call" | custom-call | flops 1000000000 | bytes 6291456 | tf_op jit(solution)/shard_map/own/pallas_call | solution.py:306
  20.9 0.6 %collective-permute-done.from_left = bf16[1808,128]{1,0:T(8,128)(2,1)S(1)} collective-permute-done((bf16[1808,128]{1,0:T(8,128)(2,1)}, bf16[1808,128]{1,0:T(8,128)(2,1)S(1)}, u32[]{:S(2)}, u32[]{:S(2)}) %collective-permute-start) | collective-permute-done | bytes 462880 | tf_op jit(solution)/shard_map/ppermute | solution.py:320
  21.6 1.0 %arrive.1 = (bf16[512,128]{1,0:T(8,128)(2,1)S(1)}, bf16[512,128]{1,0:T(8,128)(2,1)S(1)}, bf16[1024,128]{1,0:T(8,128)(2,1)S(1)}, f32[64,128]{1,0:T(8,128)S(1)}, f32[64,128]{1,0:T(8,128)S(1)}) custom-call(s32[64]{0:T(128)S(1)} %copy-done.6, s32[64]{0:T(128)S(1)} %copy-done.8, f32[64,128]{1,0:T(8,128)S(1)} %get-tuple-element.25.cap_own, ...), custom_call_target="tpu_custom_call" | custom-call | tf_op jit(solution)/shard_map/arrive/pallas_call | solution.py:306
  22.6 0.6 %collective-permute-start.2 = (bf16[512,128]{1,0:T(8,128)(2,1)S(1)}, bf16[512,128]{1,0:T(8,128)(2,1)S(1)}, u32[]{:S(2)}, u32[]{:S(2)}) collective-permute-start(bf16[512,128]{1,0:T(8,128)(2,1)S(1)} %get-tuple-element.35.below), channel_id=1, source_target_pairs={{0,1},{1,2},{2,3},{3,0},{4,5},{5,6},{6,7},{7,4},{8,9},{9,10},{10,1... | collective-permute-start | bytes 393224 | tf_op jit(solution)/shard_map/ppermute | solution.py:320
  23.2 1.5 %collective-permute-start.3 = (bf16[512,128]{1,0:T(8,128)(2,1)S(1)}, bf16[512,128]{1,0:T(8,128)(2,1)S(1)}, u32[]{:S(2)}, u32[]{:S(2)}) collective-permute-start(bf16[512,128]{1,0:T(8,128)(2,1)S(1)} %get-tuple-element.34.above), channel_id=1, source_target_pairs={{0,3},{1,0},{2,1},{3,2},{4,7},{5,4},{6,5},{7,6},{8,11},{9,8},{10,9... | collective-permute-start | bytes 393224 | tf_op jit(solution)/shard_map/ppermute | solution.py:320
  24.8 3.7 %first.1 = (bf16[6208,128]{1,0:T(8,128)(2,1)}, bf16[4096,128]{1,0:T(8,128)(2,1)S(1)}, f32[1024,128]{1,0:T(8,128)S(1)}, bf16[3072,128]{1,0:T(8,128)(2,1)S(1)}, bf16[3072,128]{1,0:T(8,128)(2,1)S(1)}) custom-call(s32[64]{0:T(128)S(1)} %copy-done.6, s32[64]{0:T(128)S(1)} %copy-done.8, s32[6,64]{1,0:T(8,128)S(1)} %bitcast.15, ...), custom_call_target="tpu_custom_call" | custom-call | flops 2000000000 | bytes 8388608 | tf_op jit(solution)/shard_map/first/pallas_call | solution.py:306
  28.5 0.9 %collective-permute-done.3.from_below = bf16[512,128]{1,0:T(8,128)(2,1)S(1)} collective-permute-done((bf16[512,128]{1,0:T(8,128)(2,1)S(1)}, bf16[512,128]{1,0:T(8,128)(2,1)S(1)}, u32[]{:S(2)}, u32[]{:S(2)}) %collective-permute-start.3) | collective-permute-done | bytes 131104 | tf_op jit(solution)/shard_map/ppermute | solution.py:320
  29.4 0.9 %ends.1 = (bf16[1024,128]{1,0:T(8,128)(2,1)S(1)}, bf16[1024,128]{1,0:T(8,128)(2,1)S(1)}, bf16[1024,128]{1,0:T(8,128)(2,1)S(1)}, bf16[512,128]{1,0:T(8,128)(2,1)S(1)}, bf16[512,128]{1,0:T(8,128)(2,1)S(1)}) custom-call(s32[6,64]{1,0:T(8,128)S(1)} %bitcast.16, f32[64,128]{1,0:T(8,128)S(1)} %get-tuple-element.31.wt, bf16[64,384]{1,0:T(8,128)(2,1)S(1)} %neg.9.faces, ...), custom_call_target="tpu_custom_call" | custom-call | tf_op jit(solution)/shard_map/ends/pallas_call | solution.py:306
  30.4 5.1 %collective-permute-start.5 = (bf16[1024,128]{1,0:T(8,128)(2,1)S(1)}, bf16[1024,128]{1,0:T(8,128)(2,1)S(1)}, u32[]{:S(2)}, u32[]{:S(2)}) collective-permute-start(bf16[1024,128]{1,0:T(8,128)(2,1)S(1)} %get-tuple-element.41.sent_left), channel_id=1, source_target_pairs={{0,252},{4,0},{8,4},{12,8},{16,12},{20,16},{24,20},{28,24},{32,28}... | collective-permute-start | bytes 786440 | tf_op jit(solution)/shard_map/ppermute | solution.py:320
  35.5 0.8 %collective-permute-start.6 = (bf16[512,128]{1,0:T(8,128)(2,1)S(1)}, bf16[512,128]{1,0:T(8,128)(2,1)S(1)}, u32[]{:S(2)}, u32[]{:S(2)}) collective-permute-start(bf16[512,128]{1,0:T(8,128)(2,1)S(1)} %get-tuple-element.43), channel_id=1, source_target_pairs={{0,1},{1,2},{2,3},{3,0},{4,5},{5,6},{6,7},{7,4},{8,9},{9,10},{10,1... | collective-permute-start | bytes 393224 | tf_op jit(solution)/shard_map/ppermute | solution.py:320
  36.3 1.2 %collective-permute-start.7 = (bf16[512,128]{1,0:T(8,128)(2,1)S(1)}, bf16[512,128]{1,0:T(8,128)(2,1)S(1)}, u32[]{:S(2)}, u32[]{:S(2)}) collective-permute-start(bf16[512,128]{1,0:T(8,128)(2,1)S(1)} %get-tuple-element.44), channel_id=1, source_target_pairs={{0,3},{1,0},{2,1},{3,2},{4,7},{5,4},{6,5},{7,6},{8,11},{9,8},{10,9... | collective-permute-start | bytes 393224 | tf_op jit(solution)/shard_map/ppermute | solution.py:320
  37.5 2.9 %collective-permute-done.6.from_above = bf16[512,128]{1,0:T(8,128)(2,1)S(1)} collective-permute-done((bf16[512,128]{1,0:T(8,128)(2,1)S(1)}, bf16[512,128]{1,0:T(8,128)(2,1)S(1)}, u32[]{:S(2)}, u32[]{:S(2)}) %collective-permute-start.6) | collective-permute-done | bytes 131104 | tf_op jit(solution)/shard_map/ppermute | solution.py:320
  40.4 2.0 %collective-permute-done.7.from_below = bf16[512,128]{1,0:T(8,128)(2,1)S(1)} collective-permute-done((bf16[512,128]{1,0:T(8,128)(2,1)S(1)}, bf16[512,128]{1,0:T(8,128)(2,1)S(1)}, u32[]{:S(2)}, u32[]{:S(2)}) %collective-permute-start.7) | collective-permute-done | bytes 131104 | tf_op jit(solution)/shard_map/ppermute | solution.py:320
  42.5 3.2 %second.1 = bf16[4096,128]{1,0:T(8,128)(2,1)} custom-call(s32[6,64]{1,0:T(8,128)S(1)} %bitcast.17, f32[64,128]{1,0:T(8,128)S(1)} %get-tuple-element.30.cap, bf16[64,384]{1,0:T(8,128)(2,1)S(1)} %neg.9.faces, bf16[4096,128]{1,0:T(8,128)(2,1)S(1)} %get-tuple-element.36.matrices, bf16[3072,128]{1,0:T(8,128)(2,1)S(1)} %get-tuple-element.37.mid, ...), custom_call_target="tpu_custom_call" | custom-call | flops 1000000000 | bytes 6291456 | tf_op jit(solution)/shard_map/second/pallas_call | solution.py:306
  (26 shorter events, 0.2 us)
Async XLA Ops:
  0.0 17.8 %copy-start.9 = (s32[1,6,64]{2,0,1:T(1,128)S(1)}, s32[1,6,64]{2,0,1:T(1,128)}, u32[]{:S(2)}) copy-start(s32[1,6,64]{2,0,1:T(1,128)} %param.12) | copy-start | bytes 4612
  0.0 1.3 %copy-start = (bf16[1,80,64,128]{3,2,1,0:T(8,128)(2,1)S(1)}, bf16[1,80,64,128]{3,2,1,0:T(8,128)(2,1)}, u32[]{:S(2)}) copy-start(bf16[1,80,64,128]{3,2,1,0:T(8,128)(2,1)} %param.8) | copy-start | bytes 3932164
  1.3 1.1 %copy-start.2 = (bf16[1,80,4096]{2,1,0:T(8,128)(2,1)S(1)}, bf16[1,80,4096]{2,1,0:T(8,128)(2,1)}, u32[]{:S(2)}) copy-start(bf16[1,80,4096]{2,1,0:T(8,128)(2,1)} %param.9) | copy-start | bytes 1966084
  2.4 0.8 %copy-start.4 = (bf16[1,80,256]{2,1,0:T(8,128)(2,1)S(1)}, bf16[1,80,256]{2,1,0:T(8,128)(2,1)}, u32[]{:S(2)}) copy-start(bf16[1,80,256]{2,1,0:T(8,128)(2,1)} %param.7) | copy-start | bytes 122884
  3.2 0.7 %copy-start.5 = (s32[64]{0:T(128)S(1)}, s32[64]{0:T(128)}, u32[]{:S(2)}) copy-start(s32[64]{0:T(128)} %sl.5) | copy-start | bytes 772
  3.9 0.7 %copy-start.7 = (s32[64]{0:T(128)S(1)}, s32[64]{0:T(128)}, u32[]{:S(2)}) copy-start(s32[64]{0:T(128)} %sr.5) | copy-start | bytes 772
  4.5 13.3 %copy-start.1 = (bf16[1,80,64,128]{3,2,1,0:T(8,128)(2,1)S(1)}, bf16[1,80,64,128]{3,2,1,0:T(8,128)(2,1)}, u32[]{:S(2)}) copy-start(bf16[1,80,64,128]{3,2,1,0:T(8,128)(2,1)} %param.8) | copy-start | bytes 3932164
  4.5 13.3 %copy-start.3 = (bf16[1,80,4096]{2,1,0:T(8,128)(2,1)S(1)}, bf16[1,80,4096]{2,1,0:T(8,128)(2,1)}, u32[]{:S(2)}) copy-start(bf16[1,80,4096]{2,1,0:T(8,128)(2,1)} %param.9) | copy-start | bytes 1966084
  7.4 14.2 %collective-permute-start = (bf16[1808,128]{1,0:T(8,128)(2,1)}, bf16[1808,128]{1,0:T(8,128)(2,1)S(1)}, u32[]{:S(2)}, u32[]{:S(2)}) collective-permute-start(bf16[1808,128]{1,0:T(8,128)(2,1)} %get-tuple-element.27), channel_id=1, source_target_pairs={{0,4},{4,8},{8,12},{12,16},{16,20},{20,24},{24,28},{28,32},{32,36}... | collective-permute-start | bytes 1388552 | tf_op jit(solution)/shard_map/ppermute | solution.py:320
  7.4 14.2 %collective-permute-start.1 = (bf16[1808,128]{1,0:T(8,128)(2,1)S(1)}, bf16[1808,128]{1,0:T(8,128)(2,1)S(1)}, u32[]{:S(2)}, u32[]{:S(2)}) collective-permute-start(bf16[1808,128]{1,0:T(8,128)(2,1)S(1)} %get-tuple-element.28), channel_id=1, source_target_pairs={{0,252},{4,0},{8,4},{12,8},{16,12},{20,16},{24,20},{28,24},{32,28}... | collective-permute-start | bytes 1388552 | tf_op jit(solution)/shard_map/ppermute | solution.py:320
  17.8 3.8 %copy-start.6 = (s32[64]{0:T(128)S(1)}, s32[64]{0:T(128)}, u32[]{:S(2)}) copy-start(s32[64]{0:T(128)} %sl.5) | copy-start | bytes 772
  17.8 3.8 %copy-start.8 = (s32[64]{0:T(128)S(1)}, s32[64]{0:T(128)}, u32[]{:S(2)}) copy-start(s32[64]{0:T(128)} %sr.5) | copy-start | bytes 772
  22.6 5.9 %collective-permute-start.2 = (bf16[512,128]{1,0:T(8,128)(2,1)S(1)}, bf16[512,128]{1,0:T(8,128)(2,1)S(1)}, u32[]{:S(2)}, u32[]{:S(2)}) collective-permute-start(bf16[512,128]{1,0:T(8,128)(2,1)S(1)} %get-tuple-element.35.below), channel_id=1, source_target_pairs={{0,1},{1,2},{2,3},{3,0},{4,5},{5,6},{6,7},{7,4},{8,9},{9,10},{10,1... | collective-permute-start | bytes 393224 | tf_op jit(solution)/shard_map/ppermute | solution.py:320
  23.2 6.2 %collective-permute-start.3 = (bf16[512,128]{1,0:T(8,128)(2,1)S(1)}, bf16[512,128]{1,0:T(8,128)(2,1)S(1)}, u32[]{:S(2)}, u32[]{:S(2)}) collective-permute-start(bf16[512,128]{1,0:T(8,128)(2,1)S(1)} %get-tuple-element.34.above), channel_id=1, source_target_pairs={{0,3},{1,0},{2,1},{3,2},{4,7},{5,4},{6,5},{7,6},{8,11},{9,8},{10,9... | collective-permute-start | bytes 393224 | tf_op jit(solution)/shard_map/ppermute | solution.py:320
  30.3 12.1 %collective-permute-start.4 = (bf16[1024,128]{1,0:T(8,128)(2,1)S(1)}, bf16[1024,128]{1,0:T(8,128)(2,1)S(1)}, u32[]{:S(2)}, u32[]{:S(2)}) collective-permute-start(bf16[1024,128]{1,0:T(8,128)(2,1)S(1)} %get-tuple-element.42.sent_right), channel_id=1, source_target_pairs={{0,4},{4,8},{8,12},{12,16},{16,20},{20,24},{24,28},{28,32},{32,36}... | collective-permute-start | bytes 786440 | tf_op jit(solution)/shard_map/ppermute | solution.py:320
  30.4 12.0 %collective-permute-start.5 = (bf16[1024,128]{1,0:T(8,128)(2,1)S(1)}, bf16[1024,128]{1,0:T(8,128)(2,1)S(1)}, u32[]{:S(2)}, u32[]{:S(2)}) collective-permute-start(bf16[1024,128]{1,0:T(8,128)(2,1)S(1)} %get-tuple-element.41.sent_left), channel_id=1, source_target_pairs={{0,252},{4,0},{8,4},{12,8},{16,12},{20,16},{24,20},{28,24},{32,28}... | collective-permute-start | bytes 786440 | tf_op jit(solution)/shard_map/ppermute | solution.py:320
  35.5 5.0 %collective-permute-start.6 = (bf16[512,128]{1,0:T(8,128)(2,1)S(1)}, bf16[512,128]{1,0:T(8,128)(2,1)S(1)}, u32[]{:S(2)}, u32[]{:S(2)}) collective-permute-start(bf16[512,128]{1,0:T(8,128)(2,1)S(1)} %get-tuple-element.43), channel_id=1, source_target_pairs={{0,1},{1,2},{2,3},{3,0},{4,5},{5,6},{6,7},{7,4},{8,9},{9,10},{10,1... | collective-permute-start | bytes 393224 | tf_op jit(solution)/shard_map/ppermute | solution.py:320
  36.3 6.2 %collective-permute-start.7 = (bf16[512,128]{1,0:T(8,128)(2,1)S(1)}, bf16[512,128]{1,0:T(8,128)(2,1)S(1)}, u32[]{:S(2)}, u32[]{:S(2)}) collective-permute-start(bf16[512,128]{1,0:T(8,128)(2,1)S(1)} %get-tuple-element.44), channel_id=1, source_target_pairs={{0,3},{1,0},{2,1},{3,2},{4,7},{5,4},{6,5},{7,6},{8,11},{9,8},{10,9... | collective-permute-start | bytes 393224 | tf_op jit(solution)/shard_map/ppermute | solution.py:320

commit v2 on v1

v2 whole, which is shorter than its diff:
```python
import jax
import jax.numpy as jnp
from jax import lax
from jax.experimental import pallas as pl
from jax.experimental.pallas import tpu as pltpu
from jax.sharding import PartitionSpec as P

P_SIZE = 64
FACES = 6
NV = 128
E_BAL = 64
MIG = 8
RIM = 16
LAYER = 8
E_DEV = 80
N_WIDE = 64
COLS = 4
HALF = P_SIZE // 2
ABOVE = E_BAL + 2 * RIM
BELOW = ABOVE + LAYER
MISSING = BELOW + LAYER

DIR_AT = RIM * P_SIZE
BLK_AT = DIR_AT + MIG * P_SIZE
SOIL_AT = BLK_AT + MIG * HALF
MESSAGE = SOIL_AT + 2 * MIG

moisture_range = 0.4
time_step = 0.5

F32 = jnp.float32
BF16 = jnp.bfloat16


def closures(pressure, inverse_entry, pore_index, conduct_sat):
    exponent = 1.0 - 1.0 / pore_index
    log_scaled = jnp.log(-inverse_entry * pressure)
    power = jnp.exp(pore_index * log_scaled)
    log_denom = jnp.log1p(power)
    saturation = jnp.exp(-exponent * log_denom)
    ratio_log = pore_index * log_scaled - log_denom
    relative = jnp.sqrt(saturation) * jnp.square(1.0 - jnp.exp(exponent * ratio_log))
    capacity = (
        moisture_range
        * inverse_entry
        * pore_index
        * exponent
        * jnp.exp((pore_index - 1.0) * log_scaled - (exponent + 1.0) * log_denom)
        / time_step
    )
    return capacity, conduct_sat * relative


def closures_by_column(soil_rows):
    cols = [jnp.transpose(soil_rows[k * NV : (k + 1) * NV]) for k in range(2)]
    fields = [cols[i // 2][i % 2 * P_SIZE : (i % 2 + 1) * P_SIZE] for i in range(4)]
    return closures(*fields)


def counts(send_left, send_right):
    t = lax.axis_index("wide")
    before = lax.rem(t + N_WIDE - 1, N_WIDE)
    after = lax.rem(t + 1, N_WIDE)
    mine_left = send_left[t]
    mine_right = send_right[t]
    arrive_left = jnp.where(t > 0, send_right[before], 0)
    arrive_right = jnp.where(t < N_WIDE - 1, send_left[after], 0)
    return mine_left, mine_right, arrive_left, arrive_right


PARITY = 4


def sides(cnt):
    return 1 - cnt[PARITY], cnt[PARITY]


def part(side, size):
    return pl.ds(pl.multiple_of(side * size, size if size % 16 == 0 else 16), size)


def moves(cnt):
    mine_left, mine_right, arrive_left, arrive_right = (cnt[i] for i in range(4))
    live = E_BAL + mine_left + mine_right - arrive_left - arrive_right
    return mine_left, mine_right, arrive_left, arrive_right, live


def rows(index, size=P_SIZE, base=0):
    if isinstance(index, int):
        return pl.ds(base + index * size, size)
    return pl.ds(pl.multiple_of(base + index * size, 16), size)


def wide_column(columns, lane):
    return jnp.broadcast_to(columns[:, lane : lane + 1], (P_SIZE, NV))


def lane_is(p):
    return (lax.broadcasted_iota(jnp.int32, (1, NV), 1) >= P_SIZE) == bool(p)


HEAD = MIG + RIM
TAIL = E_DEV - 40
BLK_TAIL = E_DEV - 32


def prepare_kernel(
    sl, sr, nbr, soil, dirs, blocks, to_pair, to_other, cap_out, wt_out, cnt, nbr_out,
    sl_s, sr_s, soil_b, soil_f, dir_head, dir_tail, blk_head, blk_tail, blk_f, message, sems,
):
    to_left = message.at[pl.ds(0, MESSAGE)]
    to_right = message.at[pl.ds(MESSAGE, MESSAGE)]
    copies = [
        pltpu.make_async_copy(source, target, sems.at[i])
        for i, (source, target) in enumerate((
            (soil, soil_b),
            (sl, sl_s),
            (sr, sr_s),
            (dirs.at[pl.ds(0, HEAD * P_SIZE)], dir_head),
            (dirs.at[pl.ds((E_DEV - TAIL) * P_SIZE, TAIL * P_SIZE)], dir_tail),
            (blocks.at[pl.ds(0, 16)], blk_head),
            (blocks.at[pl.ds(E_DEV - BLK_TAIL, BLK_TAIL)], blk_tail),
            (nbr, nbr_out),
        ))
    ]
    for copy in copies:
        copy.start()
    for k in range(2):
        soil_f[k * NV + E_DEV : (k + 1) * NV, :] = jnp.full((NV - E_DEV, NV), 1.0, F32)
    copies[0].wait()
    for k in range(2):
        soil_f[k * NV : k * NV + E_DEV, :] = soil_b[:, k * NV : (k + 1) * NV].astype(F32)
    capacity, weight = closures_by_column(soil_f[...])
    wt_out[...] = weight
    cap_out[...] = capacity
    copies[1].wait()
    copies[2].wait()
    for i, n in enumerate(counts(sl_s, sr_s)):
        cnt[i] = n
    cnt[PARITY] = lax.rem(lax.axis_index("wide"), 2)
    mine_left, mine_right, arrive_left, arrive_right, live = moves(cnt)
    middle = mine_left - arrive_left
    tail = live - MIG
    here = pltpu.roll(weight, lax.rem(NV - middle, NV), 1)
    copies[3].wait()
    copies[4].wait()
    for i in range(RIM):
        s = middle + E_BAL - RIM + i - (E_DEV - TAIL)
        to_right[rows(i), :] = (wide_column(here, E_BAL - RIM + i) * dir_tail[rows(s), :].astype(F32)).astype(BF16)
        s = jnp.maximum(middle + i, 0)
        to_left[rows(i), :] = (wide_column(here, i) * dir_head[rows(s), :].astype(F32)).astype(BF16)
    at = pl.multiple_of((tail - (E_DEV - TAIL)) * P_SIZE, P_SIZE)
    to_right[pl.ds(DIR_AT, MIG * P_SIZE), :] = dir_tail[pl.ds(at, MIG * P_SIZE), :]
    to_left[pl.ds(DIR_AT, MIG * P_SIZE), :] = dir_head[0 : MIG * P_SIZE, :]
    for out, first in ((to_right, tail), (to_left, 0)):
        both = jnp.concatenate([soil_f[pl.ds(k * NV + first, MIG), :] for k in range(2)], 0)
        out[pl.ds(SOIL_AT, 2 * MIG), :] = both.astype(BF16)
    copies[5].wait()
    copies[6].wait()
    start = E_DEV - BLK_TAIL
    group = jnp.minimum(lax.div(tail - start, 16) * 16, BLK_TAIL - 32)
    for g in range(3):
        for c in range(HALF):
            lanes = slice(c * NV, (c + 1) * NV)
            if g == 0:
                x = blk_head[:, lanes]
            else:
                x = blk_tail[pl.ds(pl.multiple_of(group + 16 * (g - 1), 16), 16), lanes]
            blk_f[pl.ds(g * 16 * HALF + c, 16, stride=HALF), :] = x.astype(F32)
    at = pl.multiple_of((16 + tail - start - group) * HALF, HALF)
    to_right[pl.ds(BLK_AT, MIG * HALF), :] = blk_f[pl.ds(at, MIG * HALF), :].astype(BF16)
    to_left[pl.ds(BLK_AT, MIG * HALF), :] = blk_f[0 : MIG * HALF, :].astype(BF16)
    for out, side in zip((to_pair, to_other), sides(cnt)):
        out[...] = message[part(side, MESSAGE), :]
    copies[7].wait()


def own_kernel(wt, dirs, blocks, face_blocks, weighted, matrices, faces, blk_f):
    for k in range(FACES):
        faces[:, k * P_SIZE : (k + 1) * P_SIZE] = -face_blocks[k]
    weight = wt[...]
    for s in range(E_DEV):
        weighted[rows(s), :] = (wide_column(weight, s) * dirs[rows(s), :].astype(F32)).astype(BF16)
    for g in range(E_DEV // 16):
        for c in range(HALF):
            x = blocks[g * 16 : (g + 1) * 16, c * NV : (c + 1) * NV].astype(F32)
            for p in range(2):
                blk_f[pl.ds(2 * c + p, 16, stride=P_SIZE), :] = jnp.where(lane_is(p), x, 0.0)
        matrices[g * 16 * P_SIZE : (g + 1) * 16 * P_SIZE, :] = blk_f[...].astype(BF16)


ARRIVED = MESSAGE - DIR_AT
BLK_IN = BLK_AT - DIR_AT
SOIL_IN = SOIL_AT - DIR_AT


def arrive_kernel(cnt, cap_own, wt_own, pair, other, own, to_above, to_below, came, cap_out, wt_out, moved, soil_f):
    mine_left, mine_right, arrive_left, arrive_right, live = moves(cnt)
    for ref, side in zip((pair, other), sides(cnt)):
        came[part(side, ARRIVED), :] = ref[DIR_AT:, :]
    soil_f[...] = jnp.full((2 * NV, NV), 1.0, F32)
    for side in range(2):
        x = came[pl.ds(side * ARRIVED + SOIL_IN, 2 * MIG), :].astype(F32)
        for k in range(2):
            soil_f[k * NV + side * MIG : k * NV + (side + 1) * MIG, :] = x[k * MIG : (k + 1) * MIG]
    capacity, weight = closures_by_column(soil_f[...])
    lane = lax.broadcasted_iota(jnp.int32, (P_SIZE, NV), 1)
    for out, mine, theirs in ((cap_out, cap_own, capacity), (wt_out, wt_own, weight)):
        middle = pltpu.roll(mine[...], lax.rem(arrive_left - mine_left + NV, NV), 1)
        left = pltpu.roll(theirs, lax.rem(arrive_left - MIG + NV, NV), 1)
        right = pltpu.roll(theirs, E_BAL - arrive_right - MIG, 1)
        out[...] = jnp.where(lane < arrive_left, left, jnp.where(lane < E_BAL - arrive_right, middle, right))
    for i in range(2 * MIG):
        raw = came[rows(i % MIG, base=i // MIG * ARRIVED), :]
        moved[rows(i), :] = (wide_column(weight, i) * raw.astype(F32)).astype(BF16)
    shift = mine_left - arrive_left
    for i in range(LAYER):
        here = own[rows(jnp.maximum(shift + i, 0)), :].astype(F32)
        came = moved[rows(jnp.minimum(MIG - arrive_left + i, MIG - 1)), :].astype(F32)
        to_above[rows(i), :] = jnp.where(i < arrive_left, came, here).astype(BF16)
        w = E_BAL - LAYER + i
        here = own[rows(shift + w), :].astype(F32)
        came = moved[rows(jnp.maximum(w - E_BAL + arrive_right, 0) + MIG), :].astype(F32)
        to_below[rows(i), :] = jnp.where(w >= E_BAL - arrive_right, came, here).astype(BF16)


def first_kernel(
    cnt, nbr, cap, wt, faces, dirs, own, matrices, came, above, below, pair, other,
    blk_out, partial, first, nxt, near, blk_f,
):
    mine_left, mine_right, arrive_left, arrive_right, live = moves(cnt)
    shift = mine_left - arrive_left
    for w in range(E_BAL):
        if w < LAYER:
            near[rows(w), :] = above[rows(w), :]
        elif w >= E_BAL - LAYER:
            near[rows(w), :] = below[rows(w - E_BAL + LAYER), :]
        else:
            near[rows(w), :] = own[rows(shift + w), :]
    for ref, side in zip((pair, other), sides(cnt)):
        at = pl.multiple_of((E_BAL + side * RIM) * P_SIZE, P_SIZE)
        near[pl.ds(at, RIM * P_SIZE), :] = ref[0 : RIM * P_SIZE, :]
    for i in range(MIG):

        @pl.when(i < mine_left)
        def _():
            near[rows(E_BAL + RIM - mine_left + i), :] = own[rows(i), :]

        @pl.when(i < mine_right)
        def _():
            near[rows(E_BAL + RIM + i), :] = own[rows(live - mine_right + i), :]

    near[rows(ABOVE), :] = jnp.zeros((P_SIZE, NV), BF16)

    for w in range(E_BAL):
        blk_out[rows(w), :] = matrices[rows(jnp.maximum(shift + w, 0)), :]
    for i in range(MIG):

        @pl.when(i < arrive_left)
        def _():
            x = came[rows(MIG - arrive_left + i, HALF, BLK_IN), :].astype(F32)
            for p in range(2):
                blk_f[pl.ds(p, HALF, stride=2), :] = jnp.where(lane_is(p), x, 0.0)
            blk_out[rows(i), :] = blk_f[...].astype(BF16)

        @pl.when(i < arrive_right)
        def _():
            x = came[rows(i, HALF, ARRIVED + BLK_IN), :].astype(F32)
            for p in range(2):
                blk_f[pl.ds(p, HALF, stride=2), :] = jnp.where(lane_is(p), x, 0.0)
            blk_out[rows(E_BAL - arrive_right + i), :] = blk_f[...].astype(BF16)

    capacity = cap[...]
    weight = wt[...]
    face_rows = faces[...]
    for w in range(E_BAL):
        vector = dirs[rows(jnp.maximum(shift + w, 0)), :].astype(F32)
        if w < MIG:
            arrived = came[rows(jnp.minimum(MIG - arrive_left + w, MIG - 1)), :].astype(F32)
            vector = jnp.where(w < arrive_left, arrived, vector)
        elif w >= E_BAL - MIG:
            arrived = came[rows(jnp.maximum(w - E_BAL + arrive_right, 0), base=ARRIVED), :].astype(F32)
            vector = jnp.where(w >= E_BAL - arrive_right, arrived, vector)
        result = wide_column(capacity, w) * vector + product(near, nbr, blk_out, face_rows, w, ABOVE, ABOVE)
        if LAYER <= w < E_BAL - LAYER:
            rounded = result.astype(BF16)
            first[rows(w - LAYER), :] = rounded
            nxt[rows(w - LAYER), :] = (wide_column(weight, w) * rounded.astype(F32)).astype(BF16)
        else:
            partial[rows(w if w < LAYER else w - E_BAL + 2 * LAYER), :] = result


def product(near, nbr, matrices, face_rows, w, limit, missing):
    mine = near[rows(w), :]
    parts = [mine, mine]
    for k in range(FACES):
        b = nbr[k, 0, w]
        b = jnp.where((b < 0) | (b >= limit), missing, b)
        parts.append(near[rows(b), :])
    lhs = jnp.concatenate([matrices[rows(w), :], face_rows], 1)
    return jnp.dot(lhs, jnp.concatenate(parts, 0), preferred_element_type=F32)


def vertical(nbr, faces, from_above, from_below, i):
    top = i < LAYER
    w = i if top else E_BAL - 2 * LAYER + i
    k = 4 if top else 5
    came = from_above if top else from_below
    inside = nbr[k, 0, w] - (ABOVE if top else BELOW)
    there = (inside >= 0) & (inside < LAYER)
    row = came[rows(jnp.clip(inside, 0, LAYER - 1)), :]
    update = jnp.dot(faces[:, k * P_SIZE : (k + 1) * P_SIZE], row, preferred_element_type=F32)
    return w, jnp.where(there, update, 0.0)


def ends_kernel(
    cnt, nbr, wt, faces, partial, from_above, from_below, nxt, first, to_pair, to_other, to_above, to_below, near, rim,
):
    weight = wt[...]
    for i in range(2 * LAYER):
        w, update = vertical(nbr, faces, from_above, from_below, i)
        rounded = (partial[rows(i), :] + update).astype(BF16)
        first[rows(i), :] = rounded
        onward = (wide_column(weight, w) * rounded.astype(F32)).astype(BF16)
        if i < LAYER:
            rim[rows(i), :] = onward
            to_above[rows(i), :] = onward
        else:
            rim[rows(RIM + i), :] = onward
            to_below[rows(i - LAYER), :] = onward
    span = LAYER * P_SIZE
    rim[span : 3 * span, :] = jnp.concatenate(
        [nxt[0:span, :], nxt[(E_BAL - 3 * LAYER) * P_SIZE : (E_BAL - 2 * LAYER) * P_SIZE, :]], 0
    )
    for out, side in zip((to_pair, to_other), sides(cnt)):
        out[...] = rim[part(side, RIM * P_SIZE), :]
    near[0:span, :] = rim[0:span, :]
    near[span : (E_BAL - LAYER) * P_SIZE, :] = nxt[...]
    near[(E_BAL - LAYER) * P_SIZE :, :] = rim[3 * span :, :]


def second_kernel(cnt, nbr, cap, faces, matrices, mid, ends, own, pair, other, out, partial, near, done, sems):
    near[0 : E_BAL * P_SIZE, :] = own[...]
    for ref, side in zip((pair, other), sides(cnt)):
        at = pl.multiple_of((E_BAL + side * RIM) * P_SIZE, P_SIZE)
        near[pl.ds(at, RIM * P_SIZE), :] = ref[...]
    near[rows(ABOVE), :] = jnp.zeros((P_SIZE, NV), BF16)
    capacity = cap[...]
    face_rows = faces[...]
    copies = []
    for w in range(E_BAL):
        outer = w if w < LAYER else w - E_BAL + 2 * LAYER
        inner = LAYER <= w < E_BAL - LAYER
        vector = mid[rows(w - LAYER), :] if inner else ends[rows(outer), :]
        result = wide_column(capacity, w) * vector.astype(F32) + product(
            near, nbr, matrices, face_rows, w, ABOVE, ABOVE
        )
        if inner:
            done[rows(w - LAYER), :] = result.astype(BF16)
            if (w - LAYER) % PIECE == PIECE - 1:
                span = (w - LAYER + 1 - PIECE) * P_SIZE
                copies.append(
                    pltpu.make_async_copy(
                        done.at[pl.ds(span, PIECE * P_SIZE)],
                        out.at[pl.ds(span + LAYER * P_SIZE, PIECE * P_SIZE)],
                        sems.at[len(copies)],
                    )
                )
                copies[-1].start()
        else:
            partial[rows(outer), :] = result
    for copy in copies:
        copy.wait()


PIECE = 16


def finish_kernel(nbr, faces, partial, from_above, from_below, begun, out, done, sems):
    copies = []
    for i in range(2 * LAYER):
        w, update = vertical(nbr, faces, from_above, from_below, i)
        done[rows(i), :] = (partial[rows(i), :] + update).astype(BF16)
        if i % LAYER == LAYER - 1:
            span = LAYER * P_SIZE
            copies.append(
                pltpu.make_async_copy(
                    done.at[pl.ds((i + 1) * P_SIZE - span, span)],
                    out.at[pl.ds((w + 1) * P_SIZE - span, span)],
                    sems.at[len(copies)],
                )
            )
            copies[-1].start()
    for copy in copies:
        copy.wait()


def smem():
    return pl.BlockSpec(memory_space=pltpu.SMEM)


def vmem():
    return pl.BlockSpec(memory_space=pltpu.VMEM)


def hbm():
    return pl.BlockSpec(memory_space=pltpu.HBM)


def pinned(x):
    return pltpu.with_memory_space_constraint(x, pltpu.HBM)


def held(n, kind=BF16):
    return pltpu.VMEM((n, NV), kind)


def call(kernel, name, ins, arrays, outs, out_specs=None, scratch=(), flops=0, moved=0, aliases=None):
    return pl.pallas_call(
        kernel,
        out_shape=outs,
        in_specs=ins,
        out_specs=out_specs or [vmem()] * len(outs),
        scratch_shapes=list(scratch),
        compiler_params=pltpu.CompilerParams(vmem_limit_bytes=20 * 2**20),
        cost_estimate=pl.CostEstimate(flops=flops, bytes_accessed=moved, transcendentals=0),
        input_output_aliases=aliases or {},
        name=name,
    )(*arrays)


def shifted(value, axis, by):
    peers = lax.axis_size(axis)
    return lax.ppermute(value, axis, [(i, (i + by) % peers) for i in range(peers)])


def swapped(value, first):
    pairs = {i: i for i in range(N_WIDE)}
    for i in range(first, N_WIDE - 1, 2):
        pairs[i], pairs[i + 1] = i + 1, i
    return lax.ppermute(value, "wide", list(pairs.items()))


def per_device(soil_state, directions, blocks, send_left, send_right, neighbours, face_blocks):
    soil = soil_state[0]
    dirs = directions.reshape(E_DEV * P_SIZE, NV)
    rows_of = blocks[0]
    column = held(P_SIZE, F32)
    layer, rim = held(LAYER * P_SIZE), held(RIM * P_SIZE)
    slots = held(E_DEV * P_SIZE)
    inner = held((E_BAL - 2 * LAYER) * P_SIZE)

    to_pair, to_other, cap_own, wt_own, cnt, nbr = call(
        prepare_kernel, "prepare", [hbm()] * 6,
        [pinned(x) for x in (send_left, send_right, jnp.swapaxes(neighbours, 0, 1), soil, dirs, rows_of)],
        (held(MESSAGE), held(MESSAGE), column, column, pltpu.SMEM((PARITY + 1,), jnp.int32), pltpu.SMEM((FACES, 1, E_BAL), jnp.int32)),
        [vmem()] * 4 + [smem()] * 2,
        (
            pltpu.SMEM((N_WIDE,), jnp.int32), pltpu.SMEM((N_WIDE,), jnp.int32),
            pltpu.VMEM((E_DEV, 2 * NV), BF16), pltpu.VMEM((2 * NV, NV), F32),
            pltpu.VMEM((HEAD * P_SIZE, NV), BF16), pltpu.VMEM((TAIL * P_SIZE, NV), BF16),
            pltpu.VMEM((16, P_SIZE * P_SIZE), BF16), pltpu.VMEM((BLK_TAIL, P_SIZE * P_SIZE), BF16),
            pltpu.VMEM((48 * HALF, NV), F32), held(2 * MESSAGE), pltpu.SemaphoreType.DMA((8,)),
        ),
    )
    pair = swapped(to_pair, 0)
    other = swapped(to_other, 1)

    own, matrices, faces = call(
        own_kernel, "own", [vmem()] * 4, (wt_own, dirs, rows_of, face_blocks),
        (slots, slots, pltpu.VMEM((P_SIZE, FACES * P_SIZE), BF16)),
        scratch=(pltpu.VMEM((16 * P_SIZE, NV), F32),),
        flops=10**9, moved=6 * 2**20,
    )

    above, below, came, cap, wt = call(
        arrive_kernel, "arrive", [smem()] + [vmem()] * 5, (cnt, cap_own, wt_own, pair, other, own),
        (layer, layer, held(2 * ARRIVED), column, column),
        scratch=(held(2 * MIG * P_SIZE), pltpu.VMEM((2 * NV, NV), F32)),
    )
    from_below = shifted(above, "narrow", -1)
    from_above = shifted(below, "narrow", 1)

    blk, partial, first, nxt = call(
        first_kernel, "first", [smem()] * 2 + [vmem()] * 11,
        (cnt, nbr, cap, wt, faces, dirs, own, matrices, came, above, below, pair, other),
        (held(E_BAL * P_SIZE), held(2 * LAYER * P_SIZE, F32), inner, inner),
        scratch=(held((ABOVE + 1) * P_SIZE), held(P_SIZE, F32)),
        flops=2 * 10**9, moved=8 * 2**20,
    )
    ends, go_pair, go_other, go_above, go_below, onward = call(
        ends_kernel, "ends", [smem()] * 2 + [vmem()] * 6, (cnt, nbr, wt, faces, partial, from_above, from_below, nxt),
        (held(2 * LAYER * P_SIZE), rim, rim, layer, layer, held(E_BAL * P_SIZE)),
        scratch=(held(2 * RIM * P_SIZE),),
    )
    pair = swapped(go_pair, 0)
    other = swapped(go_other, 1)
    came_below = shifted(go_above, "narrow", -1)
    came_above = shifted(go_below, "narrow", 1)
    result = jax.ShapeDtypeStruct((E_BAL * P_SIZE, NV), BF16)
    begun, partial = call(
        second_kernel, "second", [smem()] * 2 + [vmem()] * 8,
        (cnt, nbr, cap, faces, blk, first, ends, onward, pair, other),
        (result, held(2 * LAYER * P_SIZE, F32)), [hbm(), vmem()],
        scratch=(
            held((ABOVE + 1) * P_SIZE), held((E_BAL - 2 * LAYER) * P_SIZE),
            pltpu.SemaphoreType.DMA(((E_BAL - 2 * LAYER) // PIECE,)),
        ),
        flops=10**9, moved=6 * 2**20,
    )
    (out,) = call(
        finish_kernel, "finish", [smem()] + [vmem()] * 4 + [hbm()],
        (nbr, faces, partial, came_above, came_below, begun),
        (result,), [hbm()],
        scratch=(held(2 * LAYER * P_SIZE), pltpu.SemaphoreType.DMA((2,))),
        aliases={5: 0},
    )
    return out.reshape(1, E_BAL, P_SIZE, NV)


def solution(mesh):
    in_specs = (
        P("narrow", "wide", None),
        P("narrow", "wide", None, None),
        P("narrow", "wide", None),
        P(),
        P(),
        P("narrow", None, "wide"),
        P(),
    )
    out_specs = P("narrow", "wide", None, None)
    return jax.shard_map(
        per_device, mesh=mesh, in_specs=in_specs, out_specs=out_specs, check_vma=False
    )
```

time: 45.9 us -> 40.2 us (0.88)
  the two profiles are of different devices: /device:TPU:6 before, /device:TPU:128 now
where the time goes in v2:
time: 40.2 us; the launch traced here: 40 us
  starting transfers between devices  14 us (35%)
  waiting for transfers between devices  13.4 us (33%)
  Pallas kernels  11.5 us (29%)
  local copies, waits for them, and re-layouts  0.9 us (2%)
    pallas_call x7, Pallas kernels, call(): pl.pallas_call(kernel, out_shape=outs, in_specs=ins, out_specs=out_specs...  11.5 us
    ppermute x4, waiting for transfers between devices, swapped(): return lax.ppermute(value, 'wide', list(pairs.items()))  9.25 us
    ppermute x4, starting transfers between devices, swapped(): return lax.ppermute(value, 'wide', list(pairs.items()))  7.87 us
    ppermute x4, starting transfers between devices, shifted(): lax.ppermute(value, axis, [(i, (i + by) % peers) for i in range(peers)])  6.15 us
    ppermute x4, waiting for transfers between devices, shifted(): lax.ppermute(value, axis, [(i, (i + by) % peers) for i in range(peers)])  4.19 us
    unnamed x6, local copies, waits for them, and re-layouts  0.9 us
  transfers between devices with their start and end apart: 8, of which 4 were waited for; matrix products, arithmetic and copies ran while one was open for 0% of the time, Pallas kernels for 18%

profile of v2, /device:TPU:128, one launch (start us, length us, event | category | flops | bytes accessed | tf_op | source)
XLA Modules:
  0.0 40.0 jit_solution(7229464657889038078)
XLA Ops:
  0.0 2.6 %prepare.1 = (bf16[1808,128]{1,0:T(8,128)(2,1)S(1)}, bf16[1808,128]{1,0:T(8,128)(2,1)S(1)}, f32[64,128]{1,0:T(8,128)S(1)}, f32[64,128]{1,0:T(8,128)S(1)}, s32[5]{0:T(128)S(4)}, /*index=5*/s32[6,1,64]{2,1,0:T(1,128)S(4)}) custom-call(s32[64]{0:T(128)} %sl.1, s32[64]{0:T(128)} %sr.1, s32[6,1,64]{2,1,0:T(1,128)} %bitcast.11, bf16[80,256]{1,0:T(8,128)(2,1)} %bitcast.10, ...), custom_call_target="tpu_custom_call" | custom-call | tf_op jit(solution)/shard_map/prepare/pallas_call | solution.py:419
  2.6 0.1 collective-permute-start
  2.7 4.6 %collective-permute-start.1 = (bf16[1808,128]{1,0:T(8,128)(2,1)S(1)}, bf16[1808,128]{1,0:T(8,128)(2,1)S(1)}, u32[]{:S(2)}, u32[]{:S(2)}) collective-permute-start(bf16[1808,128]{1,0:T(8,128)(2,1)S(1)} %get-tuple-element.37), channel_id=1, source_target_pairs={{0,0},{4,8},{8,4},{12,16},{16,12},{20,24},{24,20},{28,32},{32,28},... | collective-permute-start | bytes 1388552 | tf_op jit(solution)/shard_map/ppermute | solution.py:441
  7.3 0.0 copy-start.2
  7.3 0.9 %copy-done.2 = bf16[6,64,64]{2,1,0:T(8,128)(2,1)S(1)} copy-done((bf16[6,64,64]{2,1,0:T(8,128)(2,1)S(1)}, bf16[6,64,64]{2,1,0:T(8,128)(2,1)}, u32[]{:S(2)}) %copy-start.2) | copy-done | bytes 49176
  8.2 3.0 %own.1 = (bf16[5120,128]{1,0:T(8,128)(2,1)S(1)}, bf16[5120,128]{1,0:T(8,128)(2,1)S(1)}, bf16[64,384]{1,0:T(8,128)(2,1)S(1)}) custom-call(f32[64,128]{1,0:T(8,128)S(1)} %get-tuple-element.32.wt.wt_own, bf16[5120,128]{1,0:T(8,128)(2,1)S(1)} %bitcast.6, bf16[80,4096]{1,0:T(8,128)(2,1)S(1)} %bitcast.9, bf16[6,64,64]{2,1,0:T(8,128)(2,1)S(1)} %copy-done.2), custom_call_target="tpu_custom_call" | custom-call | flops 1000000000 | bytes 6291456 | tf_op jit(solution)/shard_map/own/pallas_call | solution.py:419
  11.1 0.0 collective-permute-done.pair
  11.2 4.7 %collective-permute-done.1.other = bf16[1808,128]{1,0:T(8,128)(2,1)S(1)} collective-permute-done((bf16[1808,128]{1,0:T(8,128)(2,1)S(1)}, bf16[1808,128]{1,0:T(8,128)(2,1)S(1)}, u32[]{:S(2)}, u32[]{:S(2)}) %collective-permute-start.1) | collective-permute-done | bytes 462880 | tf_op jit(solution)/shard_map/ppermute | solution.py:441
  15.8 0.5 %arrive.1 = (bf16[512,128]{1,0:T(8,128)(2,1)S(1)}, bf16[512,128]{1,0:T(8,128)(2,1)S(1)}, bf16[1568,128]{1,0:T(8,128)(2,1)S(1)}, f32[64,128]{1,0:T(8,128)S(1)}, f32[64,128]{1,0:T(8,128)S(1)}) custom-call(s32[5]{0:T(128)S(4)} %get-tuple-element.34.cnt, f32[64,128]{1,0:T(8,128)S(1)} %get-tuple-element.35.cap_own, f32[64,128]{1,0:T(8,128)S(1)} %get-tuple-element.32.wt.wt_own, ...), custom_call_target="tpu_custom_call" | custom-call | tf_op jit(solution)/shard_map/arrive/pallas_call | solution.py:419
  16.4 2.8 %collective-permute-start.3 = (bf16[512,128]{1,0:T(8,128)(2,1)S(1)}, bf16[512,128]{1,0:T(8,128)(2,1)S(1)}, u32[]{:S(2)}, u32[]{:S(2)}) collective-permute-start(bf16[512,128]{1,0:T(8,128)(2,1)S(1)} %get-tuple-element.43.above), channel_id=1, source_target_pairs={{0,3},{1,0},{2,1},{3,2},{4,7},{5,4},{6,5},{7,6},{8,11},{9,8},{10,9... | collective-permute-start | bytes 393224 | tf_op jit(solution)/shard_map/ppermute | solution.py:434
  19.2 0.0 collective-permute-start.2
  19.2 2.0 %first.1 = (bf16[4096,128]{1,0:T(8,128)(2,1)S(1)}, f32[1024,128]{1,0:T(8,128)S(1)}, bf16[3072,128]{1,0:T(8,128)(2,1)S(1)}, bf16[3072,128]{1,0:T(8,128)(2,1)S(1)}) custom-call(s32[5]{0:T(128)S(4)} %get-tuple-element.34.cnt, s32[6,1,64]{2,1,0:T(1,128)S(4)} %get-tuple-element.31.nbr, f32[64,128]{1,0:T(8,128)S(1)} %get-tuple-element.39.cap, ...), custom_call_target="tpu_custom_call" | custom-call | flops 2000000000 | bytes 8388608 | tf_op jit(solution)/shard_map/first/pallas_call | solution.py:419
  21.2 0.5 %collective-permute-done.3.from_below = bf16[512,128]{1,0:T(8,128)(2,1)S(1)} collective-permute-done((bf16[512,128]{1,0:T(8,128)(2,1)S(1)}, bf16[512,128]{1,0:T(8,128)(2,1)S(1)}, u32[]{:S(2)}, u32[]{:S(2)}) %collective-permute-start.3) | collective-permute-done | bytes 131104 | tf_op jit(solution)/shard_map/ppermute | solution.py:434
  21.7 3.7 %collective-permute-done.2.from_above = bf16[512,128]{1,0:T(8,128)(2,1)S(1)} collective-permute-done((bf16[512,128]{1,0:T(8,128)(2,1)S(1)}, bf16[512,128]{1,0:T(8,128)(2,1)S(1)}, u32[]{:S(2)}, u32[]{:S(2)}) %collective-permute-start.2) | collective-permute-done | bytes 131104 | tf_op jit(solution)/shard_map/ppermute | solution.py:434
  25.4 0.4 %ends.1 = (bf16[1024,128]{1,0:T(8,128)(2,1)S(1)}, bf16[1024,128]{1,0:T(8,128)(2,1)S(1)}, bf16[1024,128]{1,0:T(8,128)(2,1)S(1)}, bf16[512,128]{1,0:T(8,128)(2,1)S...) custom-call(s32[5]{0:T(128)S(4)} %get-tuple-element.34.cnt, s32[6,1,64]{2,1,0:T(1,128)S(4)} %get-tuple-element.31.nbr, ...), custom_call_target="tpu_custom_call" | custom-call | tf_op jit(solution)/shard_map/ends/pallas_call | solution.py:419
  25.8 0.1 collective-permute-start.4
  25.9 3.1 %collective-permute-start.5 = (bf16[1024,128]{1,0:T(8,128)(2,1)S(1)}, bf16[1024,128]{1,0:T(8,128)(2,1)S(1)}, u32[]{:S(2)}, u32[]{:S(2)}) collective-permute-start(bf16[1024,128]{1,0:T(8,128)(2,1)S(1)} %get-tuple-element.52), channel_id=1, source_target_pairs={{0,0},{4,8},{8,4},{12,16},{16,12},{20,24},{24,20},{28,32},{32,28},... | collective-permute-start | bytes 786440 | tf_op jit(solution)/shard_map/ppermute | solution.py:441
  29.1 0.1 collective-permute-start.6
  29.2 3.2 %collective-permute-start.7 = (bf16[512,128]{1,0:T(8,128)(2,1)S(1)}, bf16[512,128]{1,0:T(8,128)(2,1)S(1)}, u32[]{:S(2)}, u32[]{:S(2)}) collective-permute-start(bf16[512,128]{1,0:T(8,128)(2,1)S(1)} %get-tuple-element.55), channel_id=1, source_target_pairs={{0,3},{1,0},{2,1},{3,2},{4,7},{5,4},{6,5},{7,6},{8,11},{9,8},{10,9... | collective-permute-start | bytes 393224 | tf_op jit(solution)/shard_map/ppermute | solution.py:434
  32.4 0.0 collective-permute-done.4.pair
  32.4 4.6 %collective-permute-done.5.other = bf16[1024,128]{1,0:T(8,128)(2,1)S(1)} collective-permute-done((bf16[1024,128]{1,0:T(8,128)(2,1)S(1)}, bf16[1024,128]{1,0:T(8,128)(2,1)S(1)}, u32[]{:S(2)}, u32[]{:S(2)}) %collective-permute-start.5) | collective-permute-done | bytes 262176 | tf_op jit(solution)/shard_map/ppermute | solution.py:441
  37.0 2.1 %second.1 = (bf16[4096,128]{1,0:T(8,128)(2,1)}, f32[1024,128]{1,0:T(8,128)S(1)}) custom-call(s32[5]{0:T(128)S(4)} %get-tuple-element.34.cnt, s32[6,1,64]{2,1,0:T(1,128)S(4)} %get-tuple-element.31.nbr, f32[64,128]{1,0:T(8,128)S(1)} %get-tuple-element.39.cap, bf16[64,384]{1,0:T(8,128)(2,1)S(1)} %get-tuple-element.33.faces, ...), custom_call_target="tpu_custom_call" | custom-call | flops 1000000000 | bytes 6291456 | tf_op jit(solution)/shard_map/second/pallas_call | solution.py:419
  39.1 0.0 collective-permute-done.7.from_below
  39.1 0.9 %finish.1 = bf16[4096,128]{1,0:T(8,128)(2,1)} custom-call(s32[6,1,64]{2,1,0:T(1,128)S(4)} %get-tuple-element.31.nbr, bf16[64,384]{1,0:T(8,128)(2,1)S(1)} %get-tuple-element.33.faces, f32[1024,128]{1,0:T(8,128)S(1)} %get-tuple-element.53.partial, bf16[512,128]{1,0:T(8,128)(2,1)S(1)} %collective-permute-done.6.from_above, ...), custom_call_target="tpu_custom_call", output_to_operand_aliasing={{}: (5, {})} | custom-call | tf_op jit(solution)/shard_map/finish/pallas_call | solution.py:419
  (5 shorter events, 0.0 us)
Async XLA Ops:
  0.0 7.2 %copy-start.1 = (bf16[1,80,4096]{2,1,0:T(8,128)(2,1)S(1)}, bf16[1,80,4096]{2,1,0:T(8,128)(2,1)}, u32[]{:S(2)}) copy-start(bf16[1,80,4096]{2,1,0:T(8,128)(2,1)} %param.9) | copy-start | bytes 1966084
  0.0 7.2 %copy-start = (bf16[1,80,64,128]{3,2,1,0:T(8,128)(2,1)S(1)}, bf16[1,80,64,128]{3,2,1,0:T(8,128)(2,1)}, u32[]{:S(2)}) copy-start(bf16[1,80,64,128]{3,2,1,0:T(8,128)(2,1)} %param.8) | copy-start | bytes 3932164
  2.6 8.6 %collective-permute-start = (bf16[1808,128]{1,0:T(8,128)(2,1)S(1)}, bf16[1808,128]{1,0:T(8,128)(2,1)S(1)}, u32[]{:S(2)}, u32[]{:S(2)}) collective-permute-start(bf16[1808,128]{1,0:T(8,128)(2,1)S(1)} %get-tuple-element.36), channel_id=1, source_target_pairs={{0,4},{4,0},{8,12},{12,8},{16,20},{20,16},{24,28},{28,24},{32,36},... | collective-permute-start | bytes 1388552 | tf_op jit(solution)/shard_map/ppermute | solution.py:441
  2.7 13.2 %collective-permute-start.1 = (bf16[1808,128]{1,0:T(8,128)(2,1)S(1)}, bf16[1808,128]{1,0:T(8,128)(2,1)S(1)}, u32[]{:S(2)}, u32[]{:S(2)}) collective-permute-start(bf16[1808,128]{1,0:T(8,128)(2,1)S(1)} %get-tuple-element.37), channel_id=1, source_target_pairs={{0,0},{4,8},{8,4},{12,16},{16,12},{20,24},{24,20},{28,32},{32,28},... | collective-permute-start | bytes 1388552 | tf_op jit(solution)/shard_map/ppermute | solution.py:441
  7.3 0.9 %copy-start.2 = (bf16[6,64,64]{2,1,0:T(8,128)(2,1)S(1)}, bf16[6,64,64]{2,1,0:T(8,128)(2,1)}, u32[]{:S(2)}) copy-start(bf16[6,64,64]{2,1,0:T(8,128)(2,1)} %face_blocks.1) | copy-start | bytes 147460
  16.4 5.4 %collective-permute-start.3 = (bf16[512,128]{1,0:T(8,128)(2,1)S(1)}, bf16[512,128]{1,0:T(8,128)(2,1)S(1)}, u32[]{:S(2)}, u32[]{:S(2)}) collective-permute-start(bf16[512,128]{1,0:T(8,128)(2,1)S(1)} %get-tuple-element.43.above), channel_id=1, source_target_pairs={{0,3},{1,0},{2,1},{3,2},{4,7},{5,4},{6,5},{7,6},{8,11},{9,8},{10,9... | collective-permute-start | bytes 393224 | tf_op jit(solution)/shard_map/ppermute | solution.py:434
  19.2 6.2 %collective-permute-start.2 = (bf16[512,128]{1,0:T(8,128)(2,1)S(1)}, bf16[512,128]{1,0:T(8,128)(2,1)S(1)}, u32[]{:S(2)}, u32[]{:S(2)}) collective-permute-start(bf16[512,128]{1,0:T(8,128)(2,1)S(1)} %get-tuple-element.44.below), channel_id=1, source_target_pairs={{0,1},{1,2},{2,3},{3,0},{4,5},{5,6},{6,7},{7,4},{8,9},{9,10},{10,1... | collective-permute-start | bytes 393224 | tf_op jit(solution)/shard_map/ppermute | solution.py:434
  25.8 6.6 %collective-permute-start.4 = (bf16[1024,128]{1,0:T(8,128)(2,1)S(1)}, bf16[1024,128]{1,0:T(8,128)(2,1)S(1)}, u32[]{:S(2)}, u32[]{:S(2)}) collective-permute-start(bf16[1024,128]{1,0:T(8,128)(2,1)S(1)} %get-tuple-element.51), channel_id=1, source_target_pairs={{0,4},{4,0},{8,12},{12,8},{16,20},{20,16},{24,28},{28,24},{32,36},... | collective-permute-start | bytes 786440 | tf_op jit(solution)/shard_map/ppermute | solution.py:441
  25.9 11.0 %collective-permute-start.5 = (bf16[1024,128]{1,0:T(8,128)(2,1)S(1)}, bf16[1024,128]{1,0:T(8,128)(2,1)S(1)}, u32[]{:S(2)}, u32[]{:S(2)}) collective-permute-start(bf16[1024,128]{1,0:T(8,128)(2,1)S(1)} %get-tuple-element.52), channel_id=1, source_target_pairs={{0,0},{4,8},{8,4},{12,16},{16,12},{20,24},{24,20},{28,32},{32,28},... | collective-permute-start | bytes 786440 | tf_op jit(solution)/shard_map/ppermute | solution.py:441
  29.1 10.0 %collective-permute-start.6 = (bf16[512,128]{1,0:T(8,128)(2,1)S(1)}, bf16[512,128]{1,0:T(8,128)(2,1)S(1)}, u32[]{:S(2)}, u32[]{:S(2)}) collective-permute-start(bf16[512,128]{1,0:T(8,128)(2,1)S(1)} %get-tuple-element.54), channel_id=1, source_target_pairs={{0,1},{1,2},{2,3},{3,0},{4,5},{5,6},{6,7},{7,4},{8,9},{9,10},{10,1... | collective-permute-start | bytes 393224 | tf_op jit(solution)/shard_map/ppermute | solution.py:434
  29.2 9.9 %collective-permute-start.7 = (bf16[512,128]{1,0:T(8,128)(2,1)S(1)}, bf16[512,128]{1,0:T(8,128)(2,1)S(1)}, u32[]{:S(2)}, u32[]{:S(2)}) collective-permute-start(bf16[512,128]{1,0:T(8,128)(2,1)S(1)} %get-tuple-element.55), channel_id=1, source_target_pairs={{0,3},{1,0},{2,1},{3,2},{4,7},{5,4},{6,5},{7,6},{8,11},{9,8},{10,9... | collective-permute-start | bytes 393224 | tf_op jit(solution)/shard_map/ppermute | solution.py:434

commit v3 on v2

--- a/solution.py
+++ b/solution.py
@@ -105,7 +105,7 @@
 
 
 def prepare_kernel(
-    sl, sr, nbr, soil, dirs, blocks, to_pair, to_other, cap_out, wt_out, cnt, nbr_out,
+    sl, sr, nbr, soil, dirs, blocks, to_other, to_pair, cap_out, wt_out, cnt, nbr_out,
     sl_s, sr_s, soil_b, soil_f, dir_head, dir_tail, blk_head, blk_tail, blk_f, message, sems,
 ):
     to_left = message.at[pl.ds(0, MESSAGE)]
@@ -194,7 +194,7 @@
 SOIL_IN = SOIL_AT - DIR_AT
 
 
-def arrive_kernel(cnt, cap_own, wt_own, pair, other, own, to_above, to_below, came, cap_out, wt_out, moved, soil_f):
+def arrive_kernel(other, pair, cnt, cap_own, wt_own, own, to_above, to_below, came, cap_out, wt_out, moved, soil_f):
     mine_left, mine_right, arrive_left, arrive_right, live = moves(cnt)
     for ref, side in zip((pair, other), sides(cnt)):
         came[part(side, ARRIVED), :] = ref[DIR_AT:, :]
@@ -314,7 +314,7 @@
 
 
 def ends_kernel(
-    cnt, nbr, wt, faces, partial, from_above, from_below, nxt, first, to_pair, to_other, to_above, to_below, near, rim,
+    cnt, nbr, wt, faces, partial, from_above, from_below, nxt, first, to_other, to_pair, to_above, to_below, near, rim,
 ):
     weight = wt[...]
     for i in range(2 * LAYER):
@@ -339,7 +339,7 @@
     near[(E_BAL - LAYER) * P_SIZE :, :] = rim[3 * span :, :]
 
 
-def second_kernel(cnt, nbr, cap, faces, matrices, mid, ends, own, pair, other, out, partial, near, done, sems):
+def second_kernel(other, pair, cnt, nbr, cap, faces, matrices, mid, ends, own, out, partial, near, done, sems):
     near[0 : E_BAL * P_SIZE, :] = own[...]
     for ref, side in zip((pair, other), sides(cnt)):
         at = pl.multiple_of((E_BAL + side * RIM) * P_SIZE, P_SIZE)
@@ -435,10 +435,13 @@
 
 
 def swapped(value, first):
-    pairs = {i: i for i in range(N_WIDE)}
-    for i in range(first, N_WIDE - 1, 2):
-        pairs[i], pairs[i + 1] = i + 1, i
-    return lax.ppermute(value, "wide", list(pairs.items()))
+    pairs = []
+    for t in range(N_WIDE):
+        partner = t + 1 if (t - first) % 2 == 0 else t - 1
+        for c in range(COLS):
+            target = (partner, c) if 0 <= partner < N_WIDE else (t, c ^ 1)
+            pairs.append((t * COLS + c, target[0] * COLS + target[1]))
+    return lax.ppermute(value, ("wide", "narrow"), pairs)
 
 
 def per_device(soil_state, directions, blocks, send_left, send_right, neighbours, face_blocks):
@@ -450,7 +453,7 @@
     slots = held(E_DEV * P_SIZE)
     inner = held((E_BAL - 2 * LAYER) * P_SIZE)
 
-    to_pair, to_other, cap_own, wt_own, cnt, nbr = call(
+    to_other, to_pair, cap_own, wt_own, cnt, nbr = call(
         prepare_kernel, "prepare", [hbm()] * 6,
         [pinned(x) for x in (send_left, send_right, jnp.swapaxes(neighbours, 0, 1), soil, dirs, rows_of)],
         (held(MESSAGE), held(MESSAGE), column, column, pltpu.SMEM((PARITY + 1,), jnp.int32), pltpu.SMEM((FACES, 1, E_BAL), jnp.int32)),
@@ -463,8 +466,8 @@
             pltpu.VMEM((48 * HALF, NV), F32), held(2 * MESSAGE), pltpu.SemaphoreType.DMA((8,)),
         ),
     )
+    other = swapped(to_other, 1)
     pair = swapped(to_pair, 0)
-    other = swapped(to_other, 1)
 
     own, matrices, faces = call(
         own_kernel, "own", [vmem()] * 4, (wt_own, dirs, rows_of, face_blocks),
@@ -474,7 +477,7 @@
     )
 
     above, below, came, cap, wt = call(
-        arrive_kernel, "arrive", [smem()] + [vmem()] * 5, (cnt, cap_own, wt_own, pair, other, own),
+        arrive_kernel, "arrive", [vmem()] * 2 + [smem()] + [vmem()] * 3, (other, pair, cnt, cap_own, wt_own, own),
         (layer, layer, held(2 * ARRIVED), column, column),
         scratch=(held(2 * MIG * P_SIZE), pltpu.VMEM((2 * NV, NV), F32)),
     )
@@ -488,19 +491,19 @@
         scratch=(held((ABOVE + 1) * P_SIZE), held(P_SIZE, F32)),
         flops=2 * 10**9, moved=8 * 2**20,
     )
-    ends, go_pair, go_other, go_above, go_below, onward = call(
+    ends, go_other, go_pair, go_above, go_below, onward = call(
         ends_kernel, "ends", [smem()] * 2 + [vmem()] * 6, (cnt, nbr, wt, faces, partial, from_above, from_below, nxt),
         (held(2 * LAYER * P_SIZE), rim, rim, layer, layer, held(E_BAL * P_SIZE)),
         scratch=(held(2 * RIM * P_SIZE),),
     )
+    other = swapped(go_other, 1)
     pair = swapped(go_pair, 0)
-    other = swapped(go_other, 1)
     came_below = shifted(go_above, "narrow", -1)
     came_above = shifted(go_below, "narrow", 1)
     result = jax.ShapeDtypeStruct((E_BAL * P_SIZE, NV), BF16)
     begun, partial = call(
-        second_kernel, "second", [smem()] * 2 + [vmem()] * 8,
-        (cnt, nbr, cap, faces, blk, first, ends, onward, pair, other),
+        second_kernel, "second", [vmem()] * 2 + [smem()] * 2 + [vmem()] * 6,
+        (other, pair, cnt, nbr, cap, faces, blk, first, ends, onward),
         (result, held(2 * LAYER * P_SIZE, F32)), [hbm(), vmem()],
         scratch=(
             held((ABOVE + 1) * P_SIZE), held((E_BAL - 2 * LAYER) * P_SIZE),

time: 40.2 us -> 36.3 us (0.903)
  starting transfers between devices: 14 us -> 8.82 us
  waiting for transfers between devices: 13.4 us -> 14.9 us
    ppermute x4, starting transfers between devices: 7.87 us -> 2.74 us  [swapped(): return lax.ppermute(value, ('wide', 'narrow'), pairs)]
    ppermute x4, waiting for transfers between devices: 9.25 us -> 10.7 us  [swapped(): return lax.ppermute(value, ('wide', 'narrow'), pairs)]
  transfers between devices with their start and end apart: 8 -> 8, of which waited for: 4 -> 4; matrix products, arithmetic and copies ran while one was open for 0% -> 0% of each run, Pallas kernels for 18% -> 20%
where the time goes in v3:
time: 36.3 us; the launch traced here: 36.2 us
  waiting for transfers between devices  14.9 us (41%)
  Pallas kernels  11.6 us (32%)
  starting transfers between devices  8.82 us (24%)
  local copies, waits for them, and re-layouts  0.9 us (2%)
    pallas_call x7, Pallas kernels, call(): pl.pallas_call(kernel, out_shape=outs, in_specs=ins, out_specs=out_specs...  11.6 us
    ppermute x4, waiting for transfers between devices, swapped(): return lax.ppermute(value, ('wide', 'narrow'), pairs)  10.7 us
    ppermute x4, starting transfers between devices, shifted(): lax.ppermute(value, axis, [(i, (i + by) % peers) for i in range(peers)])  6.08 us
    ppermute x4, waiting for transfers between devices, shifted(): lax.ppermute(value, axis, [(i, (i + by) % peers) for i in range(peers)])  4.17 us
    ppermute x4, starting transfers between devices, swapped(): return lax.ppermute(value, ('wide', 'narrow'), pairs)  2.74 us
    unnamed x6, local copies, waits for them, and re-layouts  0.9 us
  transfers between devices with their start and end apart: 8, of which 4 were waited for; matrix products, arithmetic and copies ran while one was open for 0% of the time, Pallas kernels for 20%

profile of v3, /device:TPU:128, one launch (start us, length us, event | category | flops | bytes accessed | tf_op | source)
XLA Modules:
  0.0 36.2 jit_solution(15316063558924332510)
XLA Ops:
  0.0 2.6 %prepare.1 = (bf16[1808,128]{1,0:T(8,128)(2,1)S(1)}, bf16[1808,128]{1,0:T(8,128)(2,1)S(1)}, f32[64,128]{1,0:T(8,128)S(1)}, f32[64,128]{1,0:T(8,128)S(1)}, s32[5]{0:T(128)S(4)}, /*index=5*/s32[6,1,64]{2,1,0:T(1,128)S(4)}) custom-call(s32[64]{0:T(128)} %sl.1, s32[64]{0:T(128)} %sr.1, s32[6,1,64]{2,1,0:T(1,128)} %bitcast.11, bf16[80,256]{1,0:T(8,128)(2,1)} %bitcast.10, ...), custom_call_target="tpu_custom_call" | custom-call | tf_op jit(solution)/shard_map/prepare/pallas_call | solution.py:419
  2.6 2.1 %collective-permute-start = (bf16[1808,128]{1,0:T(8,128)(2,1)S(1)}, bf16[1808,128]{1,0:T(8,128)(2,1)S(1)}, u32[]{:S(2)}, u32[]{:S(2)}) collective-permute-start(bf16[1808,128]{1,0:T(8,128)(2,1)S(1)} %get-tuple-element.35), channel_id=1, source_target_pairs={{0,1},{1,0},{2,3},{3,2},{4,8},{5,9},{6,10},{7,11},{8,4},{9,5},{10,... | collective-permute-start | bytes 1388552 | tf_op jit(solution)/shard_map/ppermute | solution.py:444
  4.7 0.0 collective-permute-start.1
  4.7 0.0 copy-start.2
  4.7 0.9 %copy-done.2 = bf16[6,64,64]{2,1,0:T(8,128)(2,1)S(1)} copy-done((bf16[6,64,64]{2,1,0:T(8,128)(2,1)S(1)}, bf16[6,64,64]{2,1,0:T(8,128)(2,1)}, u32[]{:S(2)}) %copy-start.2) | copy-done | bytes 49176
  5.6 3.0 %own.1 = (bf16[5120,128]{1,0:T(8,128)(2,1)S(1)}, bf16[5120,128]{1,0:T(8,128)(2,1)S(1)}, bf16[64,384]{1,0:T(8,128)(2,1)S(1)}) custom-call(f32[64,128]{1,0:T(8,128)S(1)} %get-tuple-element.32.wt.wt_own, bf16[5120,128]{1,0:T(8,128)(2,1)S(1)} %bitcast.6, bf16[80,4096]{1,0:T(8,128)(2,1)S(1)} %bitcast.9, bf16[6,64,64]{2,1,0:T(8,128)(2,1)S(1)} %copy-done.2), custom_call_target="tpu_custom_call" | custom-call | flops 1000000000 | bytes 6291456 | tf_op jit(solution)/shard_map/own/pallas_call | solution.py:419
  8.6 5.4 %collective-permute-done.other = bf16[1808,128]{1,0:T(8,128)(2,1)S(1)} collective-permute-done((bf16[1808,128]{1,0:T(8,128)(2,1)S(1)}, bf16[1808,128]{1,0:T(8,128)(2,1)S(1)}, u32[]{:S(2)}, u32[]{:S(2)}) %collective-permute-start) | collective-permute-done | bytes 462880 | tf_op jit(solution)/shard_map/ppermute | solution.py:444
  13.9 0.0 collective-permute-done.1.pair
  13.9 0.5 %arrive.1 = (bf16[512,128]{1,0:T(8,128)(2,1)S(1)}, bf16[512,128]{1,0:T(8,128)(2,1)S(1)}, bf16[1568,128]{1,0:T(8,128)(2,1)S(1)}, f32[64,128]{1,0:T(8,128)S(1)}, f32[64,128]{1,0:T(8,128)S(1)}) custom-call(bf16[1808,128]{1,0:T(8,128)(2,1)S(1)} %collective-permute-done.other, bf16[1808,128]{1,0:T(8,128)(2,1)S(1)} %collective-permute-done.1.pair, ...), custom_call_target="tpu_custom_call" | custom-call | tf_op jit(solution)/shard_map/arrive/pallas_call | solution.py:419
  14.5 2.8 %collective-permute-start.3 = (bf16[512,128]{1,0:T(8,128)(2,1)S(1)}, bf16[512,128]{1,0:T(8,128)(2,1)S(1)}, u32[]{:S(2)}, u32[]{:S(2)}) collective-permute-start(bf16[512,128]{1,0:T(8,128)(2,1)S(1)} %get-tuple-element.43.above), channel_id=1, source_target_pairs={{0,3},{1,0},{2,1},{3,2},{4,7},{5,4},{6,5},{7,6},{8,11},{9,8},{10,9... | collective-permute-start | bytes 393224 | tf_op jit(solution)/shard_map/ppermute | solution.py:434
  17.3 0.0 collective-permute-start.2
  17.3 2.0 %first.1 = (bf16[4096,128]{1,0:T(8,128)(2,1)S(1)}, f32[1024,128]{1,0:T(8,128)S(1)}, bf16[3072,128]{1,0:T(8,128)(2,1)S(1)}, bf16[3072,128]{1,0:T(8,128)(2,1)S(1)}) custom-call(s32[5]{0:T(128)S(4)} %get-tuple-element.34.cnt, s32[6,1,64]{2,1,0:T(1,128)S(4)} %get-tuple-element.31.nbr, f32[64,128]{1,0:T(8,128)S(1)} %get-tuple-element.40.cap, ...), custom_call_target="tpu_custom_call" | custom-call | flops 2000000000 | bytes 8388608 | tf_op jit(solution)/shard_map/first/pallas_call | solution.py:419
  19.3 0.5 %collective-permute-done.3.from_below = bf16[512,128]{1,0:T(8,128)(2,1)S(1)} collective-permute-done((bf16[512,128]{1,0:T(8,128)(2,1)S(1)}, bf16[512,128]{1,0:T(8,128)(2,1)S(1)}, u32[]{:S(2)}, u32[]{:S(2)}) %collective-permute-start.3) | collective-permute-done | bytes 131104 | tf_op jit(solution)/shard_map/ppermute | solution.py:434
  19.8 3.7 %collective-permute-done.2.from_above = bf16[512,128]{1,0:T(8,128)(2,1)S(1)} collective-permute-done((bf16[512,128]{1,0:T(8,128)(2,1)S(1)}, bf16[512,128]{1,0:T(8,128)(2,1)S(1)}, u32[]{:S(2)}, u32[]{:S(2)}) %collective-permute-start.2) | collective-permute-done | bytes 131104 | tf_op jit(solution)/shard_map/ppermute | solution.py:434
  23.5 0.4 %ends.1 = (bf16[1024,128]{1,0:T(8,128)(2,1)S(1)}, bf16[1024,128]{1,0:T(8,128)(2,1)S(1)}, bf16[1024,128]{1,0:T(8,128)(2,1)S(1)}, bf16[512,128]{1,0:T(8,128)(2,1)S...) custom-call(s32[5]{0:T(128)S(4)} %get-tuple-element.34.cnt, s32[6,1,64]{2,1,0:T(1,128)S(4)} %get-tuple-element.31.nbr, ...), custom_call_target="tpu_custom_call" | custom-call | tf_op jit(solution)/shard_map/ends/pallas_call | solution.py:419
  23.9 0.7 %collective-permute-start.4 = (bf16[1024,128]{1,0:T(8,128)(2,1)S(1)}, bf16[1024,128]{1,0:T(8,128)(2,1)S(1)}, u32[]{:S(2)}, u32[]{:S(2)}) collective-permute-start(bf16[1024,128]{1,0:T(8,128)(2,1)S(1)} %get-tuple-element.47), channel_id=1, source_target_pairs={{0,1},{1,0},{2,3},{3,2},{4,8},{5,9},{6,10},{7,11},{8,4},{9,5},{10,... | collective-permute-start | bytes 786440 | tf_op jit(solution)/shard_map/ppermute | solution.py:444
  24.6 0.0 collective-permute-start.5
  24.6 0.0 collective-permute-start.6
  24.6 3.2 %collective-permute-start.7 = (bf16[512,128]{1,0:T(8,128)(2,1)S(1)}, bf16[512,128]{1,0:T(8,128)(2,1)S(1)}, u32[]{:S(2)}, u32[]{:S(2)}) collective-permute-start(bf16[512,128]{1,0:T(8,128)(2,1)S(1)} %get-tuple-element.55), channel_id=1, source_target_pairs={{0,3},{1,0},{2,1},{3,2},{4,7},{5,4},{6,5},{7,6},{8,11},{9,8},{10,9... | collective-permute-start | bytes 393224 | tf_op jit(solution)/shard_map/ppermute | solution.py:434
  27.8 5.3 %collective-permute-done.4.other = bf16[1024,128]{1,0:T(8,128)(2,1)S(1)} collective-permute-done((bf16[1024,128]{1,0:T(8,128)(2,1)S(1)}, bf16[1024,128]{1,0:T(8,128)(2,1)S(1)}, u32[]{:S(2)}, u32[]{:S(2)}) %collective-permute-start.4) | collective-permute-done | bytes 262176 | tf_op jit(solution)/shard_map/ppermute | solution.py:444
  33.1 2.1 %second.1 = (bf16[4096,128]{1,0:T(8,128)(2,1)}, f32[1024,128]{1,0:T(8,128)S(1)}) custom-call(bf16[1024,128]{1,0:T(8,128)(2,1)S(1)} %collective-permute-done.4.other, bf16[1024,128]{1,0:T(8,128)(2,1)S(1)} %collective-permute-done.5.pair, s32[5]{0:T(128)S(4)} %get-tuple-element.34.cnt, s32[6,1,64]{2,1,0:T(1,128)S(4)} %get-tuple-element.31.nbr, ...), custom_call_target="tpu_custom_call" | custom-call | flops 1000000000 | bytes 6291456 | tf_op jit(solution)/shard_map/second/pallas_call | solution.py:419
  35.3 0.0 collective-permute-done.6.from_above
  35.3 0.0 collective-permute-done.7.from_below
  35.3 0.9 %finish.1 = bf16[4096,128]{1,0:T(8,128)(2,1)} custom-call(s32[6,1,64]{2,1,0:T(1,128)S(4)} %get-tuple-element.31.nbr, bf16[64,384]{1,0:T(8,128)(2,1)S(1)} %get-tuple-element.33.faces, f32[1024,128]{1,0:T(8,128)S(1)} %get-tuple-element.53.partial, bf16[512,128]{1,0:T(8,128)(2,1)S(1)} %collective-permute-done.6.from_above, ...), custom_call_target="tpu_custom_call", output_to_operand_aliasing={{}: (5, {})} | custom-call | tf_op jit(solution)/shard_map/finish/pallas_call | solution.py:419
  (5 shorter events, 0.0 us)
Async XLA Ops:
  0.0 4.7 %copy-start.1 = (bf16[1,80,4096]{2,1,0:T(8,128)(2,1)S(1)}, bf16[1,80,4096]{2,1,0:T(8,128)(2,1)}, u32[]{:S(2)}) copy-start(bf16[1,80,4096]{2,1,0:T(8,128)(2,1)} %param.9) | copy-start | bytes 1966084
  0.0 4.7 %copy-start = (bf16[1,80,64,128]{3,2,1,0:T(8,128)(2,1)S(1)}, bf16[1,80,64,128]{3,2,1,0:T(8,128)(2,1)}, u32[]{:S(2)}) copy-start(bf16[1,80,64,128]{3,2,1,0:T(8,128)(2,1)} %param.8) | copy-start | bytes 3932164
  2.6 11.4 %collective-permute-start = (bf16[1808,128]{1,0:T(8,128)(2,1)S(1)}, bf16[1808,128]{1,0:T(8,128)(2,1)S(1)}, u32[]{:S(2)}, u32[]{:S(2)}) collective-permute-start(bf16[1808,128]{1,0:T(8,128)(2,1)S(1)} %get-tuple-element.35), channel_id=1, source_target_pairs={{0,1},{1,0},{2,3},{3,2},{4,8},{5,9},{6,10},{7,11},{8,4},{9,5},{10,... | collective-permute-start | bytes 1388552 | tf_op jit(solution)/shard_map/ppermute | solution.py:444
  4.7 9.3 %collective-permute-start.1 = (bf16[1808,128]{1,0:T(8,128)(2,1)S(1)}, bf16[1808,128]{1,0:T(8,128)(2,1)S(1)}, u32[]{:S(2)}, u32[]{:S(2)}) collective-permute-start(bf16[1808,128]{1,0:T(8,128)(2,1)S(1)} %get-tuple-element.36), channel_id=1, source_target_pairs={{0,4},{1,5},{2,6},{3,7},{4,0},{5,1},{6,2},{7,3},{8,12},{9,13},{10,... | collective-permute-start | bytes 1388552 | tf_op jit(solution)/shard_map/ppermute | solution.py:444
  4.7 0.9 %copy-start.2 = (bf16[6,64,64]{2,1,0:T(8,128)(2,1)S(1)}, bf16[6,64,64]{2,1,0:T(8,128)(2,1)}, u32[]{:S(2)}) copy-start(bf16[6,64,64]{2,1,0:T(8,128)(2,1)} %face_blocks.1) | copy-start | bytes 147460
  14.5 5.4 %collective-permute-start.3 = (bf16[512,128]{1,0:T(8,128)(2,1)S(1)}, bf16[512,128]{1,0:T(8,128)(2,1)S(1)}, u32[]{:S(2)}, u32[]{:S(2)}) collective-permute-start(bf16[512,128]{1,0:T(8,128)(2,1)S(1)} %get-tuple-element.43.above), channel_id=1, source_target_pairs={{0,3},{1,0},{2,1},{3,2},{4,7},{5,4},{6,5},{7,6},{8,11},{9,8},{10,9... | collective-permute-start | bytes 393224 | tf_op jit(solution)/shard_map/ppermute | solution.py:434
  17.3 6.2 %collective-permute-start.2 = (bf16[512,128]{1,0:T(8,128)(2,1)S(1)}, bf16[512,128]{1,0:T(8,128)(2,1)S(1)}, u32[]{:S(2)}, u32[]{:S(2)}) collective-permute-start(bf16[512,128]{1,0:T(8,128)(2,1)S(1)} %get-tuple-element.44.below), channel_id=1, source_target_pairs={{0,1},{1,2},{2,3},{3,0},{4,5},{5,6},{6,7},{7,4},{8,9},{9,10},{10,1... | collective-permute-start | bytes 393224 | tf_op jit(solution)/shard_map/ppermute | solution.py:434
  23.9 9.2 %collective-permute-start.4 = (bf16[1024,128]{1,0:T(8,128)(2,1)S(1)}, bf16[1024,128]{1,0:T(8,128)(2,1)S(1)}, u32[]{:S(2)}, u32[]{:S(2)}) collective-permute-start(bf16[1024,128]{1,0:T(8,128)(2,1)S(1)} %get-tuple-element.47), channel_id=1, source_target_pairs={{0,1},{1,0},{2,3},{3,2},{4,8},{5,9},{6,10},{7,11},{8,4},{9,5},{10,... | collective-permute-start | bytes 786440 | tf_op jit(solution)/shard_map/ppermute | solution.py:444
  24.6 8.6 %collective-permute-start.5 = (bf16[1024,128]{1,0:T(8,128)(2,1)S(1)}, bf16[1024,128]{1,0:T(8,128)(2,1)S(1)}, u32[]{:S(2)}, u32[]{:S(2)}) collective-permute-start(bf16[1024,128]{1,0:T(8,128)(2,1)S(1)} %get-tuple-element.48), channel_id=1, source_target_pairs={{0,4},{1,5},{2,6},{3,7},{4,0},{5,1},{6,2},{7,3},{8,12},{9,13},{10,... | collective-permute-start | bytes 786440 | tf_op jit(solution)/shard_map/ppermute | solution.py:444
  24.6 10.7 %collective-permute-start.6 = (bf16[512,128]{1,0:T(8,128)(2,1)S(1)}, bf16[512,128]{1,0:T(8,128)(2,1)S(1)}, u32[]{:S(2)}, u32[]{:S(2)}) collective-permute-start(bf16[512,128]{1,0:T(8,128)(2,1)S(1)} %get-tuple-element.54), channel_id=1, source_target_pairs={{0,1},{1,2},{2,3},{3,0},{4,5},{5,6},{6,7},{7,4},{8,9},{9,10},{10,1... | collective-permute-start | bytes 393224 | tf_op jit(solution)/shard_map/ppermute | solution.py:434
  24.6 10.7 %collective-permute-start.7 = (bf16[512,128]{1,0:T(8,128)(2,1)S(1)}, bf16[512,128]{1,0:T(8,128)(2,1)S(1)}, u32[]{:S(2)}, u32[]{:S(2)}) collective-permute-start(bf16[512,128]{1,0:T(8,128)(2,1)S(1)} %get-tuple-element.55), channel_id=1, source_target_pairs={{0,3},{1,0},{2,1},{3,2},{4,7},{5,4},{6,5},{7,6},{8,11},{9,8},{10,9... | collective-permute-start | bytes 393224 | tf_op jit(solution)/shard_map/ppermute | solution.py:434

commit v4 on v3

--- a/solution.py
+++ b/solution.py
@@ -99,6 +99,7 @@
     return (lax.broadcasted_iota(jnp.int32, (1, NV), 1) >= P_SIZE) == bool(p)
 
 
+PITCH = HALF + 1
 HEAD = MIG + RIM
 TAIL = E_DEV - 40
 BLK_TAIL = E_DEV - 32
@@ -166,10 +167,11 @@
                 x = blk_head[:, lanes]
             else:
                 x = blk_tail[pl.ds(pl.multiple_of(group + 16 * (g - 1), 16), 16), lanes]
-            blk_f[pl.ds(g * 16 * HALF + c, 16, stride=HALF), :] = x.astype(F32)
-    at = pl.multiple_of((16 + tail - start - group) * HALF, HALF)
-    to_right[pl.ds(BLK_AT, MIG * HALF), :] = blk_f[pl.ds(at, MIG * HALF), :].astype(BF16)
-    to_left[pl.ds(BLK_AT, MIG * HALF), :] = blk_f[0 : MIG * HALF, :].astype(BF16)
+            blk_f[pl.ds(g * 16 * PITCH + c, 16, stride=PITCH), :] = x.astype(F32)
+    for i in range(MIG):
+        at = (16 + tail - start - group + i) * PITCH
+        to_right[rows(i, HALF, BLK_AT), :] = blk_f[pl.ds(at, HALF), :].astype(BF16)
+        to_left[rows(i, HALF, BLK_AT), :] = blk_f[pl.ds(i * PITCH, HALF), :].astype(BF16)
     for out, side in zip((to_pair, to_other), sides(cnt)):
         out[...] = message[part(side, MESSAGE), :]
     copies[7].wait()
@@ -185,8 +187,9 @@
         for c in range(HALF):
             x = blocks[g * 16 : (g + 1) * 16, c * NV : (c + 1) * NV].astype(F32)
             for p in range(2):
-                blk_f[pl.ds(2 * c + p, 16, stride=P_SIZE), :] = jnp.where(lane_is(p), x, 0.0)
-        matrices[g * 16 * P_SIZE : (g + 1) * 16 * P_SIZE, :] = blk_f[...].astype(BF16)
+                blk_f[pl.ds(2 * c + p, 16, stride=P_SIZE + 1), :] = jnp.where(lane_is(p), x, 0.0)
+        for e in range(16):
+            matrices[rows(g * 16 + e), :] = blk_f[pl.ds(e * (P_SIZE + 1), P_SIZE), :].astype(BF16)
 
 
 ARRIVED = MESSAGE - DIR_AT
@@ -463,7 +466,7 @@
             pltpu.VMEM((E_DEV, 2 * NV), BF16), pltpu.VMEM((2 * NV, NV), F32),
             pltpu.VMEM((HEAD * P_SIZE, NV), BF16), pltpu.VMEM((TAIL * P_SIZE, NV), BF16),
             pltpu.VMEM((16, P_SIZE * P_SIZE), BF16), pltpu.VMEM((BLK_TAIL, P_SIZE * P_SIZE), BF16),
-            pltpu.VMEM((48 * HALF, NV), F32), held(2 * MESSAGE), pltpu.SemaphoreType.DMA((8,)),
+            held(48 * PITCH, F32), held(2 * MESSAGE), pltpu.SemaphoreType.DMA((8,)),
         ),
     )
     other = swapped(to_other, 1)
@@ -472,7 +475,7 @@
     own, matrices, faces = call(
         own_kernel, "own", [vmem()] * 4, (wt_own, dirs, rows_of, face_blocks),
         (slots, slots, pltpu.VMEM((P_SIZE, FACES * P_SIZE), BF16)),
-        scratch=(pltpu.VMEM((16 * P_SIZE, NV), F32),),
+        scratch=(held(16 * (P_SIZE + 1), F32),),
         flops=10**9, moved=6 * 2**20,
     )
 

time: 36.3 us -> 35.7 us (0.983)
  Pallas kernels: 11.6 us -> 9.14 us
  waiting for transfers between devices: 14.9 us -> 16.7 us
    pallas_call x7, Pallas kernels: 11.6 us -> 9.14 us  [call(): pl.pallas_call(kernel, out_shape=outs, in_specs=ins, out_specs=out_specs...]
    ppermute x4, waiting for transfers between devices: 10.7 us -> 12.5 us  [swapped(): return lax.ppermute(value, ('wide', 'narrow'), pairs)]
  transfers between devices with their start and end apart: 8 -> 8, of which waited for: 4 -> 4; matrix products, arithmetic and copies ran while one was open for 0% -> 0% of each run, Pallas kernels for 20% -> 15%
where the time goes in v4:
time: 35.7 us; the launch traced here: 35.6 us
  waiting for transfers between devices  16.7 us (47%)
  Pallas kernels  9.14 us (26%)
  starting transfers between devices  8.82 us (25%)
  local copies, waits for them, and re-layouts  0.9 us (3%)
    ppermute x4, waiting for transfers between devices, swapped(): return lax.ppermute(value, ('wide', 'narrow'), pairs)  12.5 us
    pallas_call x7, Pallas kernels, call(): pl.pallas_call(kernel, out_shape=outs, in_specs=ins, out_specs=out_specs...  9.14 us
    ppermute x4, starting transfers between devices, shifted(): lax.ppermute(value, axis, [(i, (i + by) % peers) for i in range(peers)])  6.08 us
    ppermute x4, waiting for transfers between devices, shifted(): lax.ppermute(value, axis, [(i, (i + by) % peers) for i in range(peers)])  4.16 us
    ppermute x4, starting transfers between devices, swapped(): return lax.ppermute(value, ('wide', 'narrow'), pairs)  2.74 us
    unnamed x6, local copies, waits for them, and re-layouts  0.9 us
  transfers between devices with their start and end apart: 8, of which 4 were waited for; matrix products, arithmetic and copies ran while one was open for 0% of the time, Pallas kernels for 15%

profile of v4, /device:TPU:128, one launch (start us, length us, event | category | flops | bytes accessed | tf_op | source)
XLA Modules:
  0.0 35.6 jit_solution(6696467070494750252)
XLA Ops:
  0.0 2.0 %prepare.1 = (bf16[1808,128]{1,0:T(8,128)(2,1)S(1)}, bf16[1808,128]{1,0:T(8,128)(2,1)S(1)}, f32[64,128]{1,0:T(8,128)S(1)}, f32[64,128]{1,0:T(8,128)S(1)}, s32[5]{0:T(128)S(4)}, /*index=5*/s32[6,1,64]{2,1,0:T(1,128)S(4)}) custom-call(s32[64]{0:T(128)} %sl.1, s32[64]{0:T(128)} %sr.1, s32[6,1,64]{2,1,0:T(1,128)} %bitcast.11, bf16[80,256]{1,0:T(8,128)(2,1)} %bitcast.10, ...), custom_call_target="tpu_custom_call" | custom-call | tf_op jit(solution)/shard_map/prepare/pallas_call | solution.py:422
  2.0 2.1 %collective-permute-start = (bf16[1808,128]{1,0:T(8,128)(2,1)S(1)}, bf16[1808,128]{1,0:T(8,128)(2,1)S(1)}, u32[]{:S(2)}, u32[]{:S(2)}) collective-permute-start(bf16[1808,128]{1,0:T(8,128)(2,1)S(1)} %get-tuple-element.35), channel_id=1, source_target_pairs={{0,1},{1,0},{2,3},{3,2},{4,8},{5,9},{6,10},{7,11},{8,4},{9,5},{10,... | collective-permute-start | bytes 1388552 | tf_op jit(solution)/shard_map/ppermute | solution.py:447
  4.1 0.0 collective-permute-start.1
  4.1 0.0 copy-start.2
  4.1 0.9 %copy-done.2 = bf16[6,64,64]{2,1,0:T(8,128)(2,1)S(1)} copy-done((bf16[6,64,64]{2,1,0:T(8,128)(2,1)S(1)}, bf16[6,64,64]{2,1,0:T(8,128)(2,1)}, u32[]{:S(2)}) %copy-start.2) | copy-done | bytes 49176
  5.0 1.2 %own.1 = (bf16[5120,128]{1,0:T(8,128)(2,1)S(1)}, bf16[5120,128]{1,0:T(8,128)(2,1)S(1)}, bf16[64,384]{1,0:T(8,128)(2,1)S(1)}) custom-call(f32[64,128]{1,0:T(8,128)S(1)} %get-tuple-element.32.wt.wt_own, bf16[5120,128]{1,0:T(8,128)(2,1)S(1)} %bitcast.6, bf16[80,4096]{1,0:T(8,128)(2,1)S(1)} %bitcast.9, bf16[6,64,64]{2,1,0:T(8,128)(2,1)S(1)} %copy-done.2), custom_call_target="tpu_custom_call" | custom-call | flops 1000000000 | bytes 6291456 | tf_op jit(solution)/shard_map/own/pallas_call | solution.py:422
  6.1 7.2 %collective-permute-done.other = bf16[1808,128]{1,0:T(8,128)(2,1)S(1)} collective-permute-done((bf16[1808,128]{1,0:T(8,128)(2,1)S(1)}, bf16[1808,128]{1,0:T(8,128)(2,1)S(1)}, u32[]{:S(2)}, u32[]{:S(2)}) %collective-permute-start) | collective-permute-done | bytes 462880 | tf_op jit(solution)/shard_map/ppermute | solution.py:447
  13.3 0.0 collective-permute-done.1.pair
  13.3 0.5 %arrive.1 = (bf16[512,128]{1,0:T(8,128)(2,1)S(1)}, bf16[512,128]{1,0:T(8,128)(2,1)S(1)}, bf16[1568,128]{1,0:T(8,128)(2,1)S(1)}, f32[64,128]{1,0:T(8,128)S(1)}, f32[64,128]{1,0:T(8,128)S(1)}) custom-call(bf16[1808,128]{1,0:T(8,128)(2,1)S(1)} %collective-permute-done.other, bf16[1808,128]{1,0:T(8,128)(2,1)S(1)} %collective-permute-done.1.pair, ...), custom_call_target="tpu_custom_call" | custom-call | tf_op jit(solution)/shard_map/arrive/pallas_call | solution.py:422
  13.9 2.8 %collective-permute-start.3 = (bf16[512,128]{1,0:T(8,128)(2,1)S(1)}, bf16[512,128]{1,0:T(8,128)(2,1)S(1)}, u32[]{:S(2)}, u32[]{:S(2)}) collective-permute-start(bf16[512,128]{1,0:T(8,128)(2,1)S(1)} %get-tuple-element.43.above), channel_id=1, source_target_pairs={{0,3},{1,0},{2,1},{3,2},{4,7},{5,4},{6,5},{7,6},{8,11},{9,8},{10,9... | collective-permute-start | bytes 393224 | tf_op jit(solution)/shard_map/ppermute | solution.py:437
  16.7 0.0 collective-permute-start.2
  16.7 2.0 %first.1 = (bf16[4096,128]{1,0:T(8,128)(2,1)S(1)}, f32[1024,128]{1,0:T(8,128)S(1)}, bf16[3072,128]{1,0:T(8,128)(2,1)S(1)}, bf16[3072,128]{1,0:T(8,128)(2,1)S(1)}) custom-call(s32[5]{0:T(128)S(4)} %get-tuple-element.34.cnt, s32[6,1,64]{2,1,0:T(1,128)S(4)} %get-tuple-element.31.nbr, f32[64,128]{1,0:T(8,128)S(1)} %get-tuple-element.40.cap, ...), custom_call_target="tpu_custom_call" | custom-call | flops 2000000000 | bytes 8388608 | tf_op jit(solution)/shard_map/first/pallas_call | solution.py:422
  18.7 0.5 %collective-permute-done.3.from_below = bf16[512,128]{1,0:T(8,128)(2,1)S(1)} collective-permute-done((bf16[512,128]{1,0:T(8,128)(2,1)S(1)}, bf16[512,128]{1,0:T(8,128)(2,1)S(1)}, u32[]{:S(2)}, u32[]{:S(2)}) %collective-permute-start.3) | collective-permute-done | bytes 131104 | tf_op jit(solution)/shard_map/ppermute | solution.py:437
  19.2 3.7 %collective-permute-done.2.from_above = bf16[512,128]{1,0:T(8,128)(2,1)S(1)} collective-permute-done((bf16[512,128]{1,0:T(8,128)(2,1)S(1)}, bf16[512,128]{1,0:T(8,128)(2,1)S(1)}, u32[]{:S(2)}, u32[]{:S(2)}) %collective-permute-start.2) | collective-permute-done | bytes 131104 | tf_op jit(solution)/shard_map/ppermute | solution.py:437
  22.9 0.4 %ends.1 = (bf16[1024,128]{1,0:T(8,128)(2,1)S(1)}, bf16[1024,128]{1,0:T(8,128)(2,1)S(1)}, bf16[1024,128]{1,0:T(8,128)(2,1)S(1)}, bf16[512,128]{1,0:T(8,128)(2,1)S...) custom-call(s32[5]{0:T(128)S(4)} %get-tuple-element.34.cnt, s32[6,1,64]{2,1,0:T(1,128)S(4)} %get-tuple-element.31.nbr, ...), custom_call_target="tpu_custom_call" | custom-call | tf_op jit(solution)/shard_map/ends/pallas_call | solution.py:422
  23.3 0.7 %collective-permute-start.4 = (bf16[1024,128]{1,0:T(8,128)(2,1)S(1)}, bf16[1024,128]{1,0:T(8,128)(2,1)S(1)}, u32[]{:S(2)}, u32[]{:S(2)}) collective-permute-start(bf16[1024,128]{1,0:T(8,128)(2,1)S(1)} %get-tuple-element.47), channel_id=1, source_target_pairs={{0,1},{1,0},{2,3},{3,2},{4,8},{5,9},{6,10},{7,11},{8,4},{9,5},{10,... | collective-permute-start | bytes 786440 | tf_op jit(solution)/shard_map/ppermute | solution.py:447
  24.0 0.0 collective-permute-start.5
  24.0 0.0 collective-permute-start.6
  24.0 3.2 %collective-permute-start.7 = (bf16[512,128]{1,0:T(8,128)(2,1)S(1)}, bf16[512,128]{1,0:T(8,128)(2,1)S(1)}, u32[]{:S(2)}, u32[]{:S(2)}) collective-permute-start(bf16[512,128]{1,0:T(8,128)(2,1)S(1)} %get-tuple-element.55), channel_id=1, source_target_pairs={{0,3},{1,0},{2,1},{3,2},{4,7},{5,4},{6,5},{7,6},{8,11},{9,8},{10,9... | collective-permute-start | bytes 393224 | tf_op jit(solution)/shard_map/ppermute | solution.py:437
  27.2 5.3 %collective-permute-done.4.other = bf16[1024,128]{1,0:T(8,128)(2,1)S(1)} collective-permute-done((bf16[1024,128]{1,0:T(8,128)(2,1)S(1)}, bf16[1024,128]{1,0:T(8,128)(2,1)S(1)}, u32[]{:S(2)}, u32[]{:S(2)}) %collective-permute-start.4) | collective-permute-done | bytes 262176 | tf_op jit(solution)/shard_map/ppermute | solution.py:447
  32.6 0.0 collective-permute-done.5.pair
  32.6 2.1 %second.1 = (bf16[4096,128]{1,0:T(8,128)(2,1)}, f32[1024,128]{1,0:T(8,128)S(1)}) custom-call(bf16[1024,128]{1,0:T(8,128)(2,1)S(1)} %collective-permute-done.4.other, bf16[1024,128]{1,0:T(8,128)(2,1)S(1)} %collective-permute-done.5.pair, s32[5]{0:T(128)S(4)} %get-tuple-element.34.cnt, s32[6,1,64]{2,1,0:T(1,128)S(4)} %get-tuple-element.31.nbr, ...), custom_call_target="tpu_custom_call" | custom-call | flops 1000000000 | bytes 6291456 | tf_op jit(solution)/shard_map/second/pallas_call | solution.py:422
  34.7 0.0 collective-permute-done.7.from_below
  34.7 0.9 %finish.1 = bf16[4096,128]{1,0:T(8,128)(2,1)} custom-call(s32[6,1,64]{2,1,0:T(1,128)S(4)} %get-tuple-element.31.nbr, bf16[64,384]{1,0:T(8,128)(2,1)S(1)} %get-tuple-element.33.faces, f32[1024,128]{1,0:T(8,128)S(1)} %get-tuple-element.53.partial, bf16[512,128]{1,0:T(8,128)(2,1)S(1)} %collective-permute-done.6.from_above, ...), custom_call_target="tpu_custom_call", output_to_operand_aliasing={{}: (5, {})} | custom-call | tf_op jit(solution)/shard_map/finish/pallas_call | solution.py:422
  (5 shorter events, 0.0 us)
Async XLA Ops:
  0.0 4.1 %copy-start.1 = (bf16[1,80,4096]{2,1,0:T(8,128)(2,1)S(1)}, bf16[1,80,4096]{2,1,0:T(8,128)(2,1)}, u32[]{:S(2)}) copy-start(bf16[1,80,4096]{2,1,0:T(8,128)(2,1)} %param.9) | copy-start | bytes 1966084
  0.0 4.1 %copy-start = (bf16[1,80,64,128]{3,2,1,0:T(8,128)(2,1)S(1)}, bf16[1,80,64,128]{3,2,1,0:T(8,128)(2,1)}, u32[]{:S(2)}) copy-start(bf16[1,80,64,128]{3,2,1,0:T(8,128)(2,1)} %param.8) | copy-start | bytes 3932164
  2.0 11.4 %collective-permute-start = (bf16[1808,128]{1,0:T(8,128)(2,1)S(1)}, bf16[1808,128]{1,0:T(8,128)(2,1)S(1)}, u32[]{:S(2)}, u32[]{:S(2)}) collective-permute-start(bf16[1808,128]{1,0:T(8,128)(2,1)S(1)} %get-tuple-element.35), channel_id=1, source_target_pairs={{0,1},{1,0},{2,3},{3,2},{4,8},{5,9},{6,10},{7,11},{8,4},{9,5},{10,... | collective-permute-start | bytes 1388552 | tf_op jit(solution)/shard_map/ppermute | solution.py:447
  4.1 9.3 %collective-permute-start.1 = (bf16[1808,128]{1,0:T(8,128)(2,1)S(1)}, bf16[1808,128]{1,0:T(8,128)(2,1)S(1)}, u32[]{:S(2)}, u32[]{:S(2)}) collective-permute-start(bf16[1808,128]{1,0:T(8,128)(2,1)S(1)} %get-tuple-element.36), channel_id=1, source_target_pairs={{0,4},{1,5},{2,6},{3,7},{4,0},{5,1},{6,2},{7,3},{8,12},{9,13},{10,... | collective-permute-start | bytes 1388552 | tf_op jit(solution)/shard_map/ppermute | solution.py:447
  4.1 0.9 %copy-start.2 = (bf16[6,64,64]{2,1,0:T(8,128)(2,1)S(1)}, bf16[6,64,64]{2,1,0:T(8,128)(2,1)}, u32[]{:S(2)}) copy-start(bf16[6,64,64]{2,1,0:T(8,128)(2,1)} %face_blocks.1) | copy-start | bytes 147460
  13.9 5.4 %collective-permute-start.3 = (bf16[512,128]{1,0:T(8,128)(2,1)S(1)}, bf16[512,128]{1,0:T(8,128)(2,1)S(1)}, u32[]{:S(2)}, u32[]{:S(2)}) collective-permute-start(bf16[512,128]{1,0:T(8,128)(2,1)S(1)} %get-tuple-element.43.above), channel_id=1, source_target_pairs={{0,3},{1,0},{2,1},{3,2},{4,7},{5,4},{6,5},{7,6},{8,11},{9,8},{10,9... | collective-permute-start | bytes 393224 | tf_op jit(solution)/shard_map/ppermute | solution.py:437
  16.7 6.2 %collective-permute-start.2 = (bf16[512,128]{1,0:T(8,128)(2,1)S(1)}, bf16[512,128]{1,0:T(8,128)(2,1)S(1)}, u32[]{:S(2)}, u32[]{:S(2)}) collective-permute-start(bf16[512,128]{1,0:T(8,128)(2,1)S(1)} %get-tuple-element.44.below), channel_id=1, source_target_pairs={{0,1},{1,2},{2,3},{3,0},{4,5},{5,6},{6,7},{7,4},{8,9},{9,10},{10,1... | collective-permute-start | bytes 393224 | tf_op jit(solution)/shard_map/ppermute | solution.py:437
  23.3 9.2 %collective-permute-start.4 = (bf16[1024,128]{1,0:T(8,128)(2,1)S(1)}, bf16[1024,128]{1,0:T(8,128)(2,1)S(1)}, u32[]{:S(2)}, u32[]{:S(2)}) collective-permute-start(bf16[1024,128]{1,0:T(8,128)(2,1)S(1)} %get-tuple-element.47), channel_id=1, source_target_pairs={{0,1},{1,0},{2,3},{3,2},{4,8},{5,9},{6,10},{7,11},{8,4},{9,5},{10,... | collective-permute-start | bytes 786440 | tf_op jit(solution)/shard_map/ppermute | solution.py:447
  24.0 8.6 %collective-permute-start.5 = (bf16[1024,128]{1,0:T(8,128)(2,1)S(1)}, bf16[1024,128]{1,0:T(8,128)(2,1)S(1)}, u32[]{:S(2)}, u32[]{:S(2)}) collective-permute-start(bf16[1024,128]{1,0:T(8,128)(2,1)S(1)} %get-tuple-element.48), channel_id=1, source_target_pairs={{0,4},{1,5},{2,6},{3,7},{4,0},{5,1},{6,2},{7,3},{8,12},{9,13},{10,... | collective-permute-start | bytes 786440 | tf_op jit(solution)/shard_map/ppermute | solution.py:447
  24.0 10.7 %collective-permute-start.6 = (bf16[512,128]{1,0:T(8,128)(2,1)S(1)}, bf16[512,128]{1,0:T(8,128)(2,1)S(1)}, u32[]{:S(2)}, u32[]{:S(2)}) collective-permute-start(bf16[512,128]{1,0:T(8,128)(2,1)S(1)} %get-tuple-element.54), channel_id=1, source_target_pairs={{0,1},{1,2},{2,3},{3,0},{4,5},{5,6},{6,7},{7,4},{8,9},{9,10},{10,1... | collective-permute-start | bytes 393224 | tf_op jit(solution)/shard_map/ppermute | solution.py:437
  24.0 10.7 %collective-permute-start.7 = (bf16[512,128]{1,0:T(8,128)(2,1)S(1)}, bf16[512,128]{1,0:T(8,128)(2,1)S(1)}, u32[]{:S(2)}, u32[]{:S(2)}) collective-permute-start(bf16[512,128]{1,0:T(8,128)(2,1)S(1)} %get-tuple-element.55), channel_id=1, source_target_pairs={{0,3},{1,0},{2,1},{3,2},{4,7},{5,4},{6,5},{7,6},{8,11},{9,8},{10,9... | collective-permute-start | bytes 393224 | tf_op jit(solution)/shard_map/ppermute | solution.py:437

commit v5 on v4

--- a/solution.py
+++ b/solution.py
@@ -342,57 +342,49 @@
     near[(E_BAL - LAYER) * P_SIZE :, :] = rim[3 * span :, :]
 
 
-def second_kernel(other, pair, cnt, nbr, cap, faces, matrices, mid, ends, own, out, partial, near, done, sems):
+def inner_kernel(pair, cnt, nbr, cap, faces, matrices, mid, ends, own, partial, near):
     near[0 : E_BAL * P_SIZE, :] = own[...]
-    for ref, side in zip((pair, other), sides(cnt)):
-        at = pl.multiple_of((E_BAL + side * RIM) * P_SIZE, P_SIZE)
-        near[pl.ds(at, RIM * P_SIZE), :] = ref[...]
+    here, there = sides(cnt)
+    at = pl.multiple_of((E_BAL + here * RIM) * P_SIZE, P_SIZE)
+    near[pl.ds(at, RIM * P_SIZE), :] = pair[...]
+    at = pl.multiple_of((E_BAL + there * RIM) * P_SIZE, P_SIZE)
+    near[pl.ds(at, RIM * P_SIZE), :] = jnp.zeros((RIM * P_SIZE, NV), BF16)
     near[rows(ABOVE), :] = jnp.zeros((P_SIZE, NV), BF16)
     capacity = cap[...]
     face_rows = faces[...]
-    copies = []
     for w in range(E_BAL):
         outer = w if w < LAYER else w - E_BAL + 2 * LAYER
         inner = LAYER <= w < E_BAL - LAYER
         vector = mid[rows(w - LAYER), :] if inner else ends[rows(outer), :]
-        result = wide_column(capacity, w) * vector.astype(F32) + product(
+        partial[rows(w), :] = wide_column(capacity, w) * vector.astype(F32) + product(
             near, nbr, matrices, face_rows, w, ABOVE, ABOVE
         )
-        if inner:
-            done[rows(w - LAYER), :] = result.astype(BF16)
-            if (w - LAYER) % PIECE == PIECE - 1:
-                span = (w - LAYER + 1 - PIECE) * P_SIZE
-                copies.append(
-                    pltpu.make_async_copy(
-                        done.at[pl.ds(span, PIECE * P_SIZE)],
-                        out.at[pl.ds(span + LAYER * P_SIZE, PIECE * P_SIZE)],
-                        sems.at[len(copies)],
-                    )
-                )
-                copies[-1].start()
-        else:
-            partial[rows(outer), :] = result
-    for copy in copies:
-        copy.wait()
-
-
-PIECE = 16
-
-
-def finish_kernel(nbr, faces, partial, from_above, from_below, begun, out, done, sems):
+
+
+PIECE = 8
+
+
+def second_kernel(other, cnt, nbr, faces, inside, from_above, from_below, out, near, done, sems):
+    near[0 : RIM * P_SIZE, :] = other[...]
+    near[rows(RIM), :] = jnp.zeros((P_SIZE, NV), BF16)
+    first = E_BAL + sides(cnt)[1] * RIM
+    sideways = faces[:, 0 : 4 * P_SIZE]
     copies = []
-    for i in range(2 * LAYER):
-        w, update = vertical(nbr, faces, from_above, from_below, i)
-        done[rows(i), :] = (partial[rows(i), :] + update).astype(BF16)
-        if i % LAYER == LAYER - 1:
-            span = LAYER * P_SIZE
-            copies.append(
-                pltpu.make_async_copy(
-                    done.at[pl.ds((i + 1) * P_SIZE - span, span)],
-                    out.at[pl.ds((w + 1) * P_SIZE - span, span)],
-                    sems.at[len(copies)],
-                )
-            )
+    for w in range(E_BAL):
+        parts = []
+        for k in range(4):
+            b = nbr[k, 0, w] - first
+            parts.append(near[rows(jnp.where((b < 0) | (b >= RIM), RIM, b)), :])
+        result = inside[rows(w), :] + jnp.dot(
+            sideways, jnp.concatenate(parts, 0), preferred_element_type=F32
+        )
+        if w < LAYER or w >= E_BAL - LAYER:
+            i = w if w < LAYER else w - E_BAL + 2 * LAYER
+            result = result + vertical(nbr, faces, from_above, from_below, i)[1]
+        done[rows(w), :] = result.astype(BF16)
+        if w % PIECE == PIECE - 1:
+            span = pl.ds((w + 1 - PIECE) * P_SIZE, PIECE * P_SIZE)
+            copies.append(pltpu.make_async_copy(done.at[span], out.at[span], sems.at[len(copies)]))
             copies[-1].start()
     for copy in copies:
         copy.wait()
@@ -504,22 +496,21 @@
     came_below = shifted(go_above, "narrow", -1)
     came_above = shifted(go_below, "narrow", 1)
     result = jax.ShapeDtypeStruct((E_BAL * P_SIZE, NV), BF16)
-    begun, partial = call(
-        second_kernel, "second", [vmem()] * 2 + [smem()] * 2 + [vmem()] * 6,
-        (other, pair, cnt, nbr, cap, faces, blk, first, ends, onward),
-        (result, held(2 * LAYER * P_SIZE, F32)), [hbm(), vmem()],
+    (inside,) = call(
+        inner_kernel, "inner", [vmem()] + [smem()] * 2 + [vmem()] * 6,
+        (pair, cnt, nbr, cap, faces, blk, first, ends, onward),
+        (held(E_BAL * P_SIZE, F32),),
+        scratch=(held((ABOVE + 1) * P_SIZE),),
+        flops=10**9, moved=6 * 2**20,
+    )
+    (out,) = call(
+        second_kernel, "second", [vmem()] + [smem()] * 2 + [vmem()] * 4,
+        (other, cnt, nbr, faces, inside, came_above, came_below),
+        (result,), [hbm()],
         scratch=(
-            held((ABOVE + 1) * P_SIZE), held((E_BAL - 2 * LAYER) * P_SIZE),
-            pltpu.SemaphoreType.DMA(((E_BAL - 2 * LAYER) // PIECE,)),
+            held((RIM + 1) * P_SIZE), held(E_BAL * P_SIZE), pltpu.SemaphoreType.DMA((E_BAL // PIECE,)),
         ),
         flops=10**9, moved=6 * 2**20,
-    )
-    (out,) = call(
-        finish_kernel, "finish", [smem()] + [vmem()] * 4 + [hbm()],
-        (nbr, faces, partial, came_above, came_below, begun),
-        (result,), [hbm()],
-        scratch=(held(2 * LAYER * P_SIZE), pltpu.SemaphoreType.DMA((2,))),
-        aliases={5: 0},
     )
     return out.reshape(1, E_BAL, P_SIZE, NV)
 

time: 35.7 us -> 34.8 us (0.975)
  waiting for transfers between devices: 16.7 us -> 15.2 us
    ppermute x4, waiting for transfers between devices: 12.5 us -> 9.29 us  [swapped(): return lax.ppermute(value, ('wide', 'narrow'), pairs)]
    ppermute x4, waiting for transfers between devices: 4.16 us -> 5.93 us  [shifted(): lax.ppermute(value, axis, [(i, (i + by) % peers) for i in range(peers)])]
  transfers between devices with their start and end apart: 8 -> 8, of which waited for: 4 -> 5; matrix products, arithmetic and copies ran while one was open for 0% -> 0% of each run, Pallas kernels for 15% -> 13%
where the time goes in v5:
time: 34.8 us; the launch traced here: 34.7 us
  waiting for transfers between devices  15.2 us (44%)
  Pallas kernels  9.47 us (27%)
  starting transfers between devices  8.91 us (26%)
  local copies, waits for them, and re-layouts  0.9 us (3%)
    pallas_call x7, Pallas kernels, call(): pl.pallas_call(kernel, out_shape=outs, in_specs=ins, out_specs=out_specs...  9.47 us
    ppermute x4, waiting for transfers between devices, swapped(): return lax.ppermute(value, ('wide', 'narrow'), pairs)  9.29 us
    ppermute x4, starting transfers between devices, shifted(): lax.ppermute(value, axis, [(i, (i + by) % peers) for i in range(peers)])  6.08 us
    ppermute x4, waiting for transfers between devices, shifted(): lax.ppermute(value, axis, [(i, (i + by) % peers) for i in range(peers)])  5.93 us
    ppermute x4, starting transfers between devices, swapped(): return lax.ppermute(value, ('wide', 'narrow'), pairs)  2.83 us
    unnamed x6, local copies, waits for them, and re-layouts  0.9 us
  transfers between devices with their start and end apart: 8, of which 5 were waited for; matrix products, arithmetic and copies ran while one was open for 0% of the time, Pallas kernels for 13%

profile of v5, /device:TPU:128, one launch (start us, length us, event | category | flops | bytes accessed | tf_op | source)
XLA Modules:
  0.0 34.7 jit_solution(15545361956231479355)
XLA Ops:
  0.0 2.0 %prepare.1 = (bf16[1808,128]{1,0:T(8,128)(2,1)S(1)}, bf16[1808,128]{1,0:T(8,128)(2,1)S(1)}, f32[64,128]{1,0:T(8,128)S(1)}, f32[64,128]{1,0:T(8,128)S(1)}, s32[5]{0:T(128)S(4)}, /*index=5*/s32[6,1,64]{2,1,0:T(1,128)S(4)}) custom-call(s32[64]{0:T(128)} %sl.1, s32[64]{0:T(128)} %sr.1, s32[6,1,64]{2,1,0:T(1,128)} %bitcast.11, bf16[80,256]{1,0:T(8,128)(2,1)} %bitcast.10, ...), custom_call_target="tpu_custom_call" | custom-call | tf_op jit(solution)/shard_map/prepare/pallas_call | solution.py:414
  2.0 2.1 %collective-permute-start = (bf16[1808,128]{1,0:T(8,128)(2,1)S(1)}, bf16[1808,128]{1,0:T(8,128)(2,1)S(1)}, u32[]{:S(2)}, u32[]{:S(2)}) collective-permute-start(bf16[1808,128]{1,0:T(8,128)(2,1)S(1)} %get-tuple-element.31), channel_id=1, source_target_pairs={{0,1},{1,0},{2,3},{3,2},{4,8},{5,9},{6,10},{7,11},{8,4},{9,5},{10,... | collective-permute-start | bytes 1388552 | tf_op jit(solution)/shard_map/ppermute | solution.py:439
  4.1 0.0 collective-permute-start.1
  4.1 0.0 copy-start.2
  4.1 0.9 %copy-done.2 = bf16[6,64,64]{2,1,0:T(8,128)(2,1)S(1)} copy-done((bf16[6,64,64]{2,1,0:T(8,128)(2,1)S(1)}, bf16[6,64,64]{2,1,0:T(8,128)(2,1)}, u32[]{:S(2)}) %copy-start.2) | copy-done | bytes 49176
  5.0 1.2 %own.1 = (bf16[5120,128]{1,0:T(8,128)(2,1)S(1)}, bf16[5120,128]{1,0:T(8,128)(2,1)S(1)}, bf16[64,384]{1,0:T(8,128)(2,1)S(1)}) custom-call(f32[64,128]{1,0:T(8,128)S(1)} %get-tuple-element.34.wt.wt_own, bf16[5120,128]{1,0:T(8,128)(2,1)S(1)} %bitcast.6, bf16[80,4096]{1,0:T(8,128)(2,1)S(1)} %bitcast.9, bf16[6,64,64]{2,1,0:T(8,128)(2,1)S(1)} %copy-done.2), custom_call_target="tpu_custom_call" | custom-call | flops 1000000000 | bytes 6291456 | tf_op jit(solution)/shard_map/own/pallas_call | solution.py:414
  6.1 7.2 %collective-permute-done.other = bf16[1808,128]{1,0:T(8,128)(2,1)S(1)} collective-permute-done((bf16[1808,128]{1,0:T(8,128)(2,1)S(1)}, bf16[1808,128]{1,0:T(8,128)(2,1)S(1)}, u32[]{:S(2)}, u32[]{:S(2)}) %collective-permute-start) | collective-permute-done | bytes 462880 | tf_op jit(solution)/shard_map/ppermute | solution.py:439
  13.3 0.0 collective-permute-done.1.pair
  13.3 0.5 %arrive.1 = (bf16[512,128]{1,0:T(8,128)(2,1)S(1)}, bf16[512,128]{1,0:T(8,128)(2,1)S(1)}, bf16[1568,128]{1,0:T(8,128)(2,1)S(1)}, f32[64,128]{1,0:T(8,128)S(1)}, f32[64,128]{1,0:T(8,128)S(1)}) custom-call(bf16[1808,128]{1,0:T(8,128)(2,1)S(1)} %collective-permute-done.other, bf16[1808,128]{1,0:T(8,128)(2,1)S(1)} %collective-permute-done.1.pair, ...), custom_call_target="tpu_custom_call" | custom-call | tf_op jit(solution)/shard_map/arrive/pallas_call | solution.py:414
  13.9 2.8 %collective-permute-start.3 = (bf16[512,128]{1,0:T(8,128)(2,1)S(1)}, bf16[512,128]{1,0:T(8,128)(2,1)S(1)}, u32[]{:S(2)}, u32[]{:S(2)}) collective-permute-start(bf16[512,128]{1,0:T(8,128)(2,1)S(1)} %get-tuple-element.41.above), channel_id=1, source_target_pairs={{0,3},{1,0},{2,1},{3,2},{4,7},{5,4},{6,5},{7,6},{8,11},{9,8},{10,9... | collective-permute-start | bytes 393224 | tf_op jit(solution)/shard_map/ppermute | solution.py:429
  16.7 0.0 collective-permute-start.2
  16.7 2.0 %first.1 = (bf16[4096,128]{1,0:T(8,128)(2,1)S(1)}, f32[1024,128]{1,0:T(8,128)S(1)}, bf16[3072,128]{1,0:T(8,128)(2,1)S(1)}, bf16[3072,128]{1,0:T(8,128)(2,1)S(1)}) custom-call(s32[5]{0:T(128)S(4)} %get-tuple-element.29.cnt, s32[6,1,64]{2,1,0:T(1,128)S(4)} %get-tuple-element.30.nbr, f32[64,128]{1,0:T(8,128)S(1)} %get-tuple-element.38.cap, ...), custom_call_target="tpu_custom_call" | custom-call | flops 2000000000 | bytes 8388608 | tf_op jit(solution)/shard_map/first/pallas_call | solution.py:414
  18.7 0.5 %collective-permute-done.3.from_below = bf16[512,128]{1,0:T(8,128)(2,1)S(1)} collective-permute-done((bf16[512,128]{1,0:T(8,128)(2,1)S(1)}, bf16[512,128]{1,0:T(8,128)(2,1)S(1)}, u32[]{:S(2)}, u32[]{:S(2)}) %collective-permute-start.3) | collective-permute-done | bytes 131104 | tf_op jit(solution)/shard_map/ppermute | solution.py:429
  19.2 3.7 %collective-permute-done.2.from_above = bf16[512,128]{1,0:T(8,128)(2,1)S(1)} collective-permute-done((bf16[512,128]{1,0:T(8,128)(2,1)S(1)}, bf16[512,128]{1,0:T(8,128)(2,1)S(1)}, u32[]{:S(2)}, u32[]{:S(2)}) %collective-permute-start.2) | collective-permute-done | bytes 131104 | tf_op jit(solution)/shard_map/ppermute | solution.py:429
  22.9 0.4 %ends.1 = (bf16[1024,128]{1,0:T(8,128)(2,1)S(1)}, bf16[1024,128]{1,0:T(8,128)(2,1)S(1)}, bf16[1024,128]{1,0:T(8,128)(2,1)S(1)}, bf16[512,128]{1,0:T(8,128)(2,1)S...) custom-call(s32[5]{0:T(128)S(4)} %get-tuple-element.29.cnt, s32[6,1,64]{2,1,0:T(1,128)S(4)} %get-tuple-element.30.nbr, ...), custom_call_target="tpu_custom_call" | custom-call | tf_op jit(solution)/shard_map/ends/pallas_call | solution.py:414
  23.3 0.1 collective-permute-start.5
  23.4 0.7 %collective-permute-start.4 = (bf16[1024,128]{1,0:T(8,128)(2,1)S(1)}, bf16[1024,128]{1,0:T(8,128)(2,1)S(1)}, u32[]{:S(2)}, u32[]{:S(2)}) collective-permute-start(bf16[1024,128]{1,0:T(8,128)(2,1)S(1)} %get-tuple-element.45), channel_id=1, source_target_pairs={{0,1},{1,0},{2,3},{3,2},{4,8},{5,9},{6,10},{7,11},{8,4},{9,5},{10,... | collective-permute-start | bytes 786440 | tf_op jit(solution)/shard_map/ppermute | solution.py:439
  24.1 0.0 collective-permute-start.6
  24.1 3.2 %collective-permute-start.7 = (bf16[512,128]{1,0:T(8,128)(2,1)S(1)}, bf16[512,128]{1,0:T(8,128)(2,1)S(1)}, u32[]{:S(2)}, u32[]{:S(2)}) collective-permute-start(bf16[512,128]{1,0:T(8,128)(2,1)S(1)} %get-tuple-element.52), channel_id=1, source_target_pairs={{0,3},{1,0},{2,1},{3,2},{4,7},{5,4},{6,5},{7,6},{8,11},{9,8},{10,9... | collective-permute-start | bytes 393224 | tf_op jit(solution)/shard_map/ppermute | solution.py:429
  27.3 0.0 collective-permute-done.5.pair
  27.3 1.5 %inner.1.inside = f32[4096,128]{1,0:T(8,128)S(1)} custom-call(bf16[1024,128]{1,0:T(8,128)(2,1)S(1)} %collective-permute-done.5.pair, s32[5]{0:T(128)S(4)} %get-tuple-element.29.cnt, s32[6,1,64]{2,1,0:T(1,128)S(4)} %get-tuple-element.30.nbr, f32[64,128]{1,0:T(8,128)S(1)} %get-tuple-element.38.cap, bf16[64,384]{1,0:T(8,128)(2,1)S(1)} %get-tuple-element.37.faces, ...), custom_call_target="tpu_custom_call" | custom-call | flops 1000000000 | bytes 6291456 | tf_op jit(solution)/shard_map/inner/pallas_call | solution.py:414
  28.8 1.7 %collective-permute-done.6.from_above = bf16[512,128]{1,0:T(8,128)(2,1)S(1)} collective-permute-done((bf16[512,128]{1,0:T(8,128)(2,1)S(1)}, bf16[512,128]{1,0:T(8,128)(2,1)S(1)}, u32[]{:S(2)}, u32[]{:S(2)}) %collective-permute-start.6) | collective-permute-done | bytes 131104 | tf_op jit(solution)/shard_map/ppermute | solution.py:429
  30.6 2.1 %collective-permute-done.4.other = bf16[1024,128]{1,0:T(8,128)(2,1)S(1)} collective-permute-done((bf16[1024,128]{1,0:T(8,128)(2,1)S(1)}, bf16[1024,128]{1,0:T(8,128)(2,1)S(1)}, u32[]{:S(2)}, u32[]{:S(2)}) %collective-permute-start.4) | collective-permute-done | bytes 262176 | tf_op jit(solution)/shard_map/ppermute | solution.py:439
  32.7 1.9 %second.1 = bf16[4096,128]{1,0:T(8,128)(2,1)} custom-call(bf16[1024,128]{1,0:T(8,128)(2,1)S(1)} %collective-permute-done.4.other, s32[5]{0:T(128)S(4)} %get-tuple-element.29.cnt, s32[6,1,64]{2,1,0:T(1,128)S(4)} %get-tuple-element.30.nbr, bf16[64,384]{1,0:T(8,128)(2,1)S(1)} %get-tuple-element.37.faces, f32[4096,128]{1,0:T(8,128)S(1)} %inner.1.inside, ...), custom_call_target="tpu_custom_call" | custom-call | flops 1000000000 | bytes 6291456 | tf_op jit(solution)/shard_map/second/pallas_call | solution.py:414
  (5 shorter events, 0.0 us)
Async XLA Ops:
  0.0 4.1 %copy-start.1 = (bf16[1,80,4096]{2,1,0:T(8,128)(2,1)S(1)}, bf16[1,80,4096]{2,1,0:T(8,128)(2,1)}, u32[]{:S(2)}) copy-start(bf16[1,80,4096]{2,1,0:T(8,128)(2,1)} %param.9) | copy-start | bytes 1966084
  0.0 4.1 %copy-start = (bf16[1,80,64,128]{3,2,1,0:T(8,128)(2,1)S(1)}, bf16[1,80,64,128]{3,2,1,0:T(8,128)(2,1)}, u32[]{:S(2)}) copy-start(bf16[1,80,64,128]{3,2,1,0:T(8,128)(2,1)} %param.8) | copy-start | bytes 3932164
  2.0 11.4 %collective-permute-start = (bf16[1808,128]{1,0:T(8,128)(2,1)S(1)}, bf16[1808,128]{1,0:T(8,128)(2,1)S(1)}, u32[]{:S(2)}, u32[]{:S(2)}) collective-permute-start(bf16[1808,128]{1,0:T(8,128)(2,1)S(1)} %get-tuple-element.31), channel_id=1, source_target_pairs={{0,1},{1,0},{2,3},{3,2},{4,8},{5,9},{6,10},{7,11},{8,4},{9,5},{10,... | collective-permute-start | bytes 1388552 | tf_op jit(solution)/shard_map/ppermute | solution.py:439
  4.1 9.3 %collective-permute-start.1 = (bf16[1808,128]{1,0:T(8,128)(2,1)S(1)}, bf16[1808,128]{1,0:T(8,128)(2,1)S(1)}, u32[]{:S(2)}, u32[]{:S(2)}) collective-permute-start(bf16[1808,128]{1,0:T(8,128)(2,1)S(1)} %get-tuple-element.32), channel_id=1, source_target_pairs={{0,4},{1,5},{2,6},{3,7},{4,0},{5,1},{6,2},{7,3},{8,12},{9,13},{10,... | collective-permute-start | bytes 1388552 | tf_op jit(solution)/shard_map/ppermute | solution.py:439
  4.1 0.9 %copy-start.2 = (bf16[6,64,64]{2,1,0:T(8,128)(2,1)S(1)}, bf16[6,64,64]{2,1,0:T(8,128)(2,1)}, u32[]{:S(2)}) copy-start(bf16[6,64,64]{2,1,0:T(8,128)(2,1)} %face_blocks.1) | copy-start | bytes 147460
  13.9 5.4 %collective-permute-start.3 = (bf16[512,128]{1,0:T(8,128)(2,1)S(1)}, bf16[512,128]{1,0:T(8,128)(2,1)S(1)}, u32[]{:S(2)}, u32[]{:S(2)}) collective-permute-start(bf16[512,128]{1,0:T(8,128)(2,1)S(1)} %get-tuple-element.41.above), channel_id=1, source_target_pairs={{0,3},{1,0},{2,1},{3,2},{4,7},{5,4},{6,5},{7,6},{8,11},{9,8},{10,9... | collective-permute-start | bytes 393224 | tf_op jit(solution)/shard_map/ppermute | solution.py:429
  16.7 6.2 %collective-permute-start.2 = (bf16[512,128]{1,0:T(8,128)(2,1)S(1)}, bf16[512,128]{1,0:T(8,128)(2,1)S(1)}, u32[]{:S(2)}, u32[]{:S(2)}) collective-permute-start(bf16[512,128]{1,0:T(8,128)(2,1)S(1)} %get-tuple-element.42.below), channel_id=1, source_target_pairs={{0,1},{1,2},{2,3},{3,0},{4,5},{5,6},{6,7},{7,4},{8,9},{9,10},{10,1... | collective-permute-start | bytes 393224 | tf_op jit(solution)/shard_map/ppermute | solution.py:429
  23.3 4.0 %collective-permute-start.5 = (bf16[1024,128]{1,0:T(8,128)(2,1)S(1)}, bf16[1024,128]{1,0:T(8,128)(2,1)S(1)}, u32[]{:S(2)}, u32[]{:S(2)}) collective-permute-start(bf16[1024,128]{1,0:T(8,128)(2,1)S(1)} %get-tuple-element.46), channel_id=1, source_target_pairs={{0,4},{1,5},{2,6},{3,7},{4,0},{5,1},{6,2},{7,3},{8,12},{9,13},{10,... | collective-permute-start | bytes 786440 | tf_op jit(solution)/shard_map/ppermute | solution.py:439
  23.4 9.2 %collective-permute-start.4 = (bf16[1024,128]{1,0:T(8,128)(2,1)S(1)}, bf16[1024,128]{1,0:T(8,128)(2,1)S(1)}, u32[]{:S(2)}, u32[]{:S(2)}) collective-permute-start(bf16[1024,128]{1,0:T(8,128)(2,1)S(1)} %get-tuple-element.45), channel_id=1, source_target_pairs={{0,1},{1,0},{2,3},{3,2},{4,8},{5,9},{6,10},{7,11},{8,4},{9,5},{10,... | collective-permute-start | bytes 786440 | tf_op jit(solution)/shard_map/ppermute | solution.py:439
  24.1 6.5 %collective-permute-start.6 = (bf16[512,128]{1,0:T(8,128)(2,1)S(1)}, bf16[512,128]{1,0:T(8,128)(2,1)S(1)}, u32[]{:S(2)}, u32[]{:S(2)}) collective-permute-start(bf16[512,128]{1,0:T(8,128)(2,1)S(1)} %get-tuple-element.51), channel_id=1, source_target_pairs={{0,1},{1,2},{2,3},{3,0},{4,5},{5,6},{6,7},{7,4},{8,9},{9,10},{10,1... | collective-permute-start | bytes 393224 | tf_op jit(solution)/shard_map/ppermute | solution.py:429
  24.1 6.5 %collective-permute-start.7 = (bf16[512,128]{1,0:T(8,128)(2,1)S(1)}, bf16[512,128]{1,0:T(8,128)(2,1)S(1)}, u32[]{:S(2)}, u32[]{:S(2)}) collective-permute-start(bf16[512,128]{1,0:T(8,128)(2,1)S(1)} %get-tuple-element.52), channel_id=1, source_target_pairs={{0,3},{1,0},{2,1},{3,2},{4,7},{5,4},{6,5},{7,6},{8,11},{9,8},{10,9... | collective-permute-start | bytes 393224 | tf_op jit(solution)/shard_map/ppermute | solution.py:429
